TPU v7x, 128 devices: a whole 4x4x4 slice. The times are simulated.
128 devices in a mesh: gx: 32 (over x, y, core), gy: 4 (over z).
Axes of the slice: x: 4, y: 4, z: 4, core: 2. Of those that a mesh axis runs over, the one named last changes fastest.
Arguments:
- conserved: float32 [5, 8, 2048, 2048], P(None, None, 'gx', 'gy'), may hold values from -6 to 6
- solid_cells: int32 [2048, 2048], P('gx', 'gy'), may hold values 0 or 1
- flux_x: float32 [5, 5], replicated, may hold values from -2.5 to 2.5
- flux_y: float32 [5, 5], replicated, may hold values from -2.5 to 2.5
- counts: int32 [128], P(('gx', 'gy')), may hold values from 1 to 576, as said below
- owner_offset: int32 [73728], P(('gx', 'gy')), may hold values from 0 to 8, as said below
- stencil_base: int32 [73728], P(('gx', 'gy')), may hold values from 0 to 31048
- weights: float32 [73728, 16], P(('gx', 'gy')), may hold values from 0 to 0.125
- ghost_cells: int32 [73728], P(('gx', 'gy')), may hold values from 0 to 32767
Outputs:
- advanced: float32 [5, 8, 2048, 2048], P(None, None, 'gx', 'gy')
Inputs may be any that keep to these rules, and one draw needn't show every extreme that they name: `owner_offset`: code k names the owner tile at offset (k // 3 - 1, k % 3 - 1) from the sender's tile. Among the 576 rows of one device each code appears exactly 64 times. Live records are the first counts[s] rows of device s. In every draw, some device that is not on the grid's edge has all its eight neighbours and itself at 576.
All inputs are finite; a program needn't handle non-finite values. No bound on the sum of `solid_cells` on one device may be relied on, other than what follows from the above.
Results may differ from a plain program's by a relative error of at most 0.000067.
Values sent between devices are 32-bit elements; how exact they have to be, the bound alone decides.
A program may use at most 128 MiB of HBM per device.

v0:
```python
import functools

import jax
import jax.numpy as jnp
import ml_dtypes
import numpy as np
from jax import lax
from jax.experimental import pallas as pl
from jax.experimental.pallas import tpu as pltpu
from jax.sharding import PartitionSpec as P

F, Z, X, Y = 5, 8, 64, 512
LANES = 128
TILES = Y // LANES
HALO = 10
XE = X + 2 * HALO
ROWS = XE * Z
DROWS = (X + 2) * Z
REC = 576
CAP = 64
SIGNS = (1.0, -1.0, -1.0, -1.0, 1.0)
F32, BF16, I32 = jnp.float32, jnp.bfloat16, jnp.int32
VMEM_BYTES = 60 * 1024 * 1024
OFFSETS = [(k // 3 - 1, k % 3 - 1) for k in range(9)]


def y_matrices(left_edge, right_edge):
    margin = 80
    ys = np.arange(-margin, Y + margin)
    inside = np.ones(ys.shape, bool)
    if left_edge:
        inside &= ys >= 0
    if right_edge:
        inside &= ys < Y
    taps = np.array([1, 6, 15, 20, 15, 6, 1], np.float64) / 64
    single = np.zeros((ys.size, ys.size))
    for offset in range(-3, 4):
        single += np.diag(np.full(ys.size - abs(offset), taps[offset + 3]), offset)
    single = single * inside[:, None] * inside[None, :]
    double = single @ single
    triple = double @ single
    return [-6.0 / 64 * single, 4.0 / 64**2 * double, -1.0 / 64**3 * triple], margin


def block_matrix(powers, margin, y_in, y_out):
    columns = []
    for power in powers:
        full = np.zeros((256, LANES))
        for lane, y in enumerate(y_out):
            if y is not None:
                full[:, lane] = power[y + margin, np.asarray(y_in) + margin]
        columns.append(full)
    return np.concatenate(columns, axis=1)


def filter_constants():
    lane = np.arange(LANES)
    found = []
    for kind in ("mid", "left", "right", "edge_left", "edge_mid", "edge_right"):
        powers, margin = y_matrices(kind.endswith("left"), kind.endswith("right"))
        if kind.startswith("edge"):
            y_in = np.concatenate([np.where(lane < 64, lane, 384 + lane), np.where(lane < 64, Y + lane, lane - 128)])
            y_out = [Y] + [None] * 126 + [-1]
        else:
            c = {"mid": 1, "left": 0, "right": 3}[kind]
            y_in = np.concatenate([128 * c + lane, np.where(lane < 64, 128 * (c + 1) + lane, 128 * (c - 1) + lane)])
            y_out = list(128 * c + lane)
        found.append(block_matrix(powers, margin, np.clip(y_in, -margin, Y + margin - 1), y_out))
    whole = np.stack(found).astype(np.float32)
    high = whole.astype(ml_dtypes.bfloat16)
    low = (whole - high.astype(np.float32)).astype(ml_dtypes.bfloat16)
    first = np.concatenate([high, high], axis=1)[:, :, :128]
    rest = np.concatenate([high, high, low], axis=1)[:, :, 128:]
    return first, rest


def lane_index(rows=8):
    return lax.broadcasted_iota(I32, (rows, LANES), 1)


def prepare_kernel(u_hbm, count_ref, code_ref, base_ref, ghost_ref, weight_ref,
                   low_ref, high_ref, left_ref, right_ref, info_ref, wide_ref, ub, sems):
    copies = [
        pltpu.make_async_copy(u_hbm.at[:, :, pl.ds(c * LANES, LANES)], ub.at[c], sems.at[c]) for c in range(TILES)
    ]
    for copy in copies:
        copy.start()
    code = code_ref[...]
    base = base_ref[...]
    ghost = ghost_ref[...]
    kinds = lax.broadcasted_iota(I32, (16, REC), 0)
    hits = (kinds == code).astype(F32)
    before = (lax.broadcasted_iota(I32, (REC, REC), 0) < lax.broadcasted_iota(I32, (REC, REC), 1)).astype(F32).astype(BF16)
    ahead = jnp.dot(hits.astype(BF16), before, preferred_element_type=F32)
    rank = jnp.sum(ahead * hits, axis=0, keepdims=True).astype(I32)
    slot = code * CAP + rank
    live = lax.broadcasted_iota(I32, (1, REC), 1) < count_ref[0, 0]
    slot = jnp.where(live, slot, REC)
    placing = (lax.broadcasted_iota(I32, (REC, REC), 0) == slot).astype(F32).astype(BF16)
    base_x = ((base.astype(F32) + 0.5) * (1.0 / (Y - 3))).astype(I32)
    base_y = base - base_x * (Y - 3)
    window = jnp.minimum(base_y // 64, 6)
    first_lane = base_y - window * 64
    ghost_y = ghost % Y
    payload_rows = [window, base_x, ghost // Y, ghost_y // LANES, ghost_y % LANES]
    row_id = lax.broadcasted_iota(I32, (8, REC), 0)
    payload = jnp.zeros((8, REC), I32)
    for row, value in enumerate(payload_rows):
        payload = jnp.where(row_id == row, value, payload)
    payload = payload.astype(F32).astype(BF16)
    across = (((1,), (1,)), ((), ()))
    for k in range(9):
        part = lax.dot_general(payload, placing[k * CAP : (k + 1) * CAP], across, preferred_element_type=F32)
        info_ref[k] = jnp.concatenate([part, jnp.zeros((8, LANES - CAP), F32)], axis=1).astype(I32)
    lanes_hit = (lax.broadcasted_iota(I32, (LANES, REC), 0) == first_lane).astype(F32).astype(BF16)
    starts = lax.dot_general(placing, lanes_hit, across, preferred_element_type=F32)
    weight = weight_ref[...]
    weight_a = weight.astype(BF16)
    left_over = weight - weight_a.astype(F32)
    weight_b = left_over.astype(BF16)
    weight_c = (left_over - weight_b.astype(F32)).astype(BF16)
    ordered = (
        jnp.dot(placing, weight_a, preferred_element_type=F32)
        + jnp.dot(placing, weight_b, preferred_element_type=F32)
        + jnp.dot(placing, weight_c, preferred_element_type=F32)
    )
    shifted = [starts] + [pltpu.roll(starts, j, 1) for j in range(1, 4)]
    for i in range(4):
        total = shifted[0] * ordered[:, 4 * i : 4 * i + 1]
        for j in range(1, 4):
            total = total + shifted[j] * ordered[:, 4 * i + j : 4 * i + j + 1]
        wide_ref[i] = total
    for copy in copies:
        copy.wait()
    lane = lane_index()

    def pack(f, carry):
        for c in range(TILES):
            for x in range(HALO):
                low_ref[f, pl.ds(x * 8, 8), pl.ds(c * LANES, LANES)] = ub[c, f, pl.ds(x, 8, stride=X), :]
                high_ref[f, pl.ds(x * 8, 8), pl.ds(c * LANES, LANES)] = ub[c, f, pl.ds(X - HALO + x, 8, stride=X), :]
        for octet in range(8):
            left = jnp.zeros((8, LANES), F32)
            right = jnp.zeros((8, LANES), F32)
            for z in range(Z):
                here = (lane // 16) == z
                row = z * X + octet * 8
                left = jnp.where(here, pltpu.roll(ub[0, f, pl.ds(row, 8), :], 16 * z, 1), left)
                right = jnp.where(
                    here, pltpu.roll(ub[TILES - 1, f, pl.ds(row, 8), :], (16 * z - (LANES - HALO)) % LANES, 1), right
                )
            left_ref[f, pl.ds(octet * 8, 8), :] = left
            right_ref[f, pl.ds(octet * 8, 8), :] = right
        return carry

    lax.fori_loop(0, F, pack, 0)


def neighbour(dx, dy):
    nx, ny = lax.axis_size("gx"), lax.axis_size("gy")
    return (lax.rem(lax.axis_index("gx") + dx + nx, nx), lax.rem(lax.axis_index("gy") + dy + ny, ny))


def greet():
    barrier = pltpu.get_barrier_semaphore()
    for dx, dy in OFFSETS:
        if (dx, dy) != (0, 0):
            pl.semaphore_signal(barrier, inc=1, device_id=neighbour(dx, dy), device_id_type=pl.DeviceIdType.MESH)
    pl.semaphore_wait(barrier, 8)


def exchange_kernel(low_ref, high_ref, left_ref, right_ref, info_ref,
                    xlo, xhi, ylo, yhi, cll, clr, chl, chr_, ghosts, send_sem, recv_sem, own_sem):
    greet()
    plan = [
        (high_ref, xlo, (1, 0)),
        (low_ref, xhi, (-1, 0)),
        (right_ref, ylo, (0, 1)),
        (left_ref, yhi, (0, -1)),
        (right_ref.at[:, pl.ds(X - 16, 16)], cll, (1, 1)),
        (left_ref.at[:, pl.ds(X - 16, 16)], clr, (1, -1)),
        (right_ref.at[:, pl.ds(0, 16)], chl, (-1, 1)),
        (left_ref.at[:, pl.ds(0, 16)], chr_, (-1, -1)),
    ]
    for k, offset in enumerate(OFFSETS):
        if k != 4:
            plan.append((info_ref.at[k], ghosts.at[k], offset))
    copies = []
    for index, (source, target, (dx, dy)) in enumerate(plan):
        copies.append(
            pltpu.make_async_remote_copy(
                src_ref=source, dst_ref=target, send_sem=send_sem.at[index], recv_sem=recv_sem.at[index],
                device_id=neighbour(dx, dy), device_id_type=pl.DeviceIdType.MESH,
            )
        )
    for copy in copies:
        copy.start()
    own = pltpu.make_async_copy(info_ref.at[4], ghosts.at[4], own_sem)
    own.start()
    own.wait()
    for copy in copies:
        copy.wait()


def record_kernel(values_ref, arrived, send_sem, recv_sem, own_sem):
    greet()
    copies = []
    for k, (dx, dy) in enumerate(OFFSETS):
        if k != 4:
            copies.append(
                pltpu.make_async_remote_copy(
                    src_ref=values_ref.at[k], dst_ref=arrived.at[k], send_sem=send_sem.at[k], recv_sem=recv_sem.at[k],
                    device_id=neighbour(dx, dy), device_id_type=pl.DeviceIdType.MESH,
                )
            )
    for copy in copies:
        copy.start()
    own = pltpu.make_async_copy(values_ref.at[4], arrived.at[4], own_sem)
    own.start()
    own.wait()
    for copy in copies:
        copy.wait()


class Binomial:
    def __init__(self):
        self.held = [None] * 6

    def push(self, value):
        for i in range(6):
            before, self.held[i] = self.held[i], value
            if before is None:
                return None
            value = before + value
        return value


def main_kernel(flags, flux_x, flux_y, info, u_hbm, solid_ref, xlo, xhi, ylo, yhi, cll, clr, chl, chr_,
                first_hbm, rest_hbm, wide_ref, section_ref, values_ref,
                ub, firsts, rests, ut, hs, hi_main, lo_main, hi_side, lo_side, vs, dg, de, sems):
    gx, gy = lax.axis_index("gx"), lax.axis_index("gy")
    last_x, last_y = lax.axis_size("gx") - 1, lax.axis_size("gy") - 1
    flag_lo, flag_hi, flag_left, flag_right = flags[0], flags[1], flags[2], flags[3]
    kinds = [
        jnp.where(gy == 0, 1, 0),
        0,
        jnp.where(gy == last_y, 2, 0),
        jnp.where(gy == 0, 3, jnp.where(gy == last_y, 5, 4)),
    ]
    copies = [
        pltpu.make_async_copy(u_hbm.at[:, :, pl.ds(c * LANES, LANES)], ub.at[c], sems.at[c]) for c in range(TILES)
    ]
    for i, kind in enumerate(kinds):
        copies.append(pltpu.make_async_copy(first_hbm.at[kind], firsts.at[i], sems.at[4 + i]))
        copies.append(pltpu.make_async_copy(rest_hbm.at[kind], rests.at[i], sems.at[8 + i]))
    for copy in copies:
        copy.start()
    for copy in copies:
        copy.wait()
    lane = lane_index()
    low_half = lane < 64

    def per_field(f, carry):
        for c in range(TILES):
            ut[c, pl.ds(0, 80), :] = xlo[f, :, pl.ds(c * LANES, LANES)] * flag_lo
            ut[c, pl.ds(ROWS - 80, 80), :] = xhi[f, :, pl.ds(c * LANES, LANES)] * flag_hi
            for x in range(X):
                ut[c, pl.ds((HALO + x) * 8, 8), :] = ub[c, f, pl.ds(x, 8, stride=X), :]
        for octet in range(-2, 10):
            if octet < 0:
                left, right = [r[f, pl.ds((octet + 2) * 8, 8), :] * flag_lo for r in (cll, clr)]
            elif octet >= 8:
                left, right = [r[f, pl.ds((octet - 8) * 8, 8), :] * flag_hi for r in (chl, chr_)]
            else:
                left, right = [r[f, pl.ds(octet * 8, 8), :] for r in (ylo, yhi)]
            left, right = left * flag_left, right * flag_right
            for z in range(Z):
                from_right = pltpu.roll(right, (-16 * z) % LANES, 1)
                from_left = pltpu.roll(left, (LANES - HALO - 16 * z) % LANES, 1)
                hs[pl.ds((octet + 2) * 64 + z, 8, stride=8), :] = jnp.where(low_half, from_right, from_left)

        keep_low = (lane_index(16) < 64).astype(F32).astype(BF16)
        keep_high = (lane_index(16) >= 64).astype(F32).astype(BF16)
        for block in range(ROWS // 16):
            rows = pl.ds(block * 16, 16)
            highs, lows = [], []
            for c in range(TILES + 1):
                value = ut[c, rows, :] if c < TILES else hs[pl.ds(block * 16 + 48, 16), :]
                high = value.astype(BF16)
                low = (value - high.astype(F32)).astype(BF16)
                highs.append(high)
                lows.append(low)
            for parts, main, side in ((highs, hi_main, hi_side), (lows, lo_main, lo_side)):
                lo_parts = [p * keep_low for p in parts]
                hi_parts = [p * keep_high for p in parts]
                for c in range(TILES):
                    main[c, rows, :] = parts[c]
                    after = lo_parts[c + 1] if c < TILES - 1 else lo_parts[TILES]
                    ahead = hi_parts[c - 1] if c > 0 else hi_parts[TILES]
                    side[c, rows, :] = after + ahead
                main[TILES, rows, :] = lo_parts[0] + hi_parts[TILES - 1]
                side[TILES, rows, :] = parts[TILES]

        for c in range(TILES + 1):
            which = (0, 1, 1, 2, 3)[c]
            high = jnp.concatenate([hi_main[c], hi_side[c]], axis=1)
            low = jnp.concatenate([lo_main[c], lo_side[c]], axis=1)
            vs[c % 2, :, pl.ds(0, 128)] = jnp.dot(
                jnp.concatenate([high, low], axis=1), firsts[which], preferred_element_type=F32
            )
            vs[c % 2, :, pl.ds(128, 256)] = jnp.dot(
                jnp.concatenate([high, low, high], axis=1), rests[which], preferred_element_type=F32
            )
            stages = [Binomial(), Binomial(), Binomial()]

            def mask(value, e):
                return value * flag_lo if e < HALO else value * flag_hi if e >= HALO + X else value

            for e in range(XE):
                value = stages[2].push(vs[c % 2, pl.ds(e * 8, 8), pl.ds(256, 128)])
                if value is None:
                    continue
                value = mask(value, e - 3) + vs[c % 2, pl.ds((e - 3) * 8, 8), pl.ds(128, 128)]
                value = stages[1].push(value)
                if value is None:
                    continue
                value = mask(value, e - 6) + vs[c % 2, pl.ds((e - 6) * 8, 8), pl.ds(0, 128)]
                value = stages[0].push(value)
                if value is None:
                    continue
                at = e - 9
                start = ut[c, pl.ds(at * 8, 8), :] if c < TILES else hs[pl.ds(at * 8 + 48, 8), :]
                value = mask(value, at) + 4.0 * start
                drows = pl.ds((at - 9) * 8, 8)
                if c == TILES:
                    de[f, drows, :] = value
                else:
                    dg[2 * c, f, drows, :] = value
        for x in range(1, X + 1):
            drows = pl.ds(x * 8, 8)
            turned = [pltpu.roll(dg[2 * c, f, drows, :], 64, 1) for c in range(TILES)]
            for c in range(TILES - 1):
                dg[2 * c + 1, f, drows, :] = jnp.where(low_half, turned[c], turned[c + 1])
        return carry

    lax.fori_loop(0, F, per_field, 0)

    def per_code(k, carry):
        def per_group(group, held):
            held = list(held)
            weights = [wide_ref[i, pl.ds(pl.multiple_of(k * CAP + group * 8, 8), 8), :] for i in range(4)]
            for j in range(8):
                slot = group * 8 + j
                window = info[k, 0, slot]
                start = pl.multiple_of((info[k, 1, slot] + 1) * 8, 8)
                rows = [jnp.broadcast_to(weights[i][j : j + 1, :], (8, LANES)) for i in range(4)]
                for f in range(F):
                    cells = dg[window, f, pl.ds(start, 32), :]
                    total = cells[0:8] * rows[0]
                    for i in range(1, 4):
                        total = total + cells[8 * i : 8 * i + 8] * rows[i]
                    value = jnp.sum(total, axis=1, keepdims=True) * SIGNS[f]
                    held[f] = jnp.where(lane == slot, value, held[f])
            return tuple(held)

        held = lax.fori_loop(0, CAP // 8, per_group, tuple(jnp.zeros((8, LANES), F32) for _ in range(F)))
        for f in range(F):
            values_ref[k, pl.ds(f * 8, 8), :] = held[f]
        return carry

    lax.fori_loop(0, 9, per_code, 0)

    def per_octet(octet, carry):
        for c in range(TILES):
            solid = solid_ref[pl.ds(pl.multiple_of(octet * 8, 8), 8), pl.ds(c * LANES, LANES)]
            for half in range(4):
                first = pl.multiple_of((octet * 8 + half * 2) * 8, 8)
                here = pl.ds(first + 8, 16)
                slopes_x, slopes_y, mids = [], [], []
                wide_lane = lane_index(16)
                for g in range(F):
                    mid = dg[2 * c, g, here, :]
                    before = dg[2 * c, g, pl.ds(first, 16), :]
                    after = dg[2 * c, g, pl.ds(first + 16, 16), :]
                    left = dg[2 * (c - 1), g, here, :] if c > 0 else de[g, here, :]
                    right = dg[2 * (c + 1), g, here, :] if c < TILES - 1 else de[g, here, :]
                    up = jnp.where(wide_lane == LANES - 1, pltpu.roll(right, LANES - 1, 1), pltpu.roll(mid, LANES - 1, 1))
                    down = jnp.where(wide_lane == 0, pltpu.roll(left, 1, 1), pltpu.roll(mid, 1, 1))
                    mids.append(mid)
                    slopes_x.append(after - before)
                    slopes_y.append(up - down)
                for f in range(F):
                    total = -0.125 * mids[f]
                    for g in range(F):
                        total = total + flux_x[f, g] * slopes_x[g] + flux_y[f, g] * slopes_y[g]
                    for i in range(2):
                        x = octet * 8 + half * 2 + i
                        cells = total[8 * i : 8 * i + 8] + 1.125 * ub[c, f, pl.ds(x, 8, stride=X), :]
                        row = half * 2 + i
                        blocked = jnp.broadcast_to(solid[row : row + 1, :], (8, LANES)) == 1
                        section_ref[c, f, pl.ds(first + 8 * i, 8), :] = jnp.where(blocked, 0.0, cells)
        return carry

    lax.fori_loop(0, X // 8, per_octet, 0)


def scatter_kernel(valid, info, section_ref, arrived, out_hbm, work, natural, sems):
    lane = lane_index()
    for c in range(TILES):
        for f in range(F):
            work[c, f] = section_ref[c, f]

    def per_code(k, carry):
        weight = valid[k]
        blocks = [arrived[k, pl.ds(f * 8, 8), :] * weight for f in range(F)]
        for j in range(CAP):
            start = pl.multiple_of(info[k, 2, j] * 8, 8)
            tile = info[k, 3, j]
            hit = lane == info[k, 4, j]
            for f in range(F):
                value = jnp.broadcast_to(blocks[f][:, j : j + 1], (8, LANES))
                rows = pl.ds(start, 8)
                work[tile, f, rows, :] = work[tile, f, rows, :] + jnp.where(hit, value, 0.0)
        return carry

    lax.fori_loop(0, 9, per_code, 0)
    copies = []
    for c in range(TILES):

        def per_field(f, carry):
            for x in range(X):
                natural[c, f, pl.ds(x, 8, stride=X), :] = work[c, f, pl.ds(x * 8, 8), :]
            return carry

        lax.fori_loop(0, F, per_field, 0)
        copy = pltpu.make_async_copy(natural.at[c], out_hbm.at[:, :, pl.ds(c * LANES, LANES)], sems.at[c])
        copy.start()
        copies.append(copy)
    for copy in copies:
        copy.wait()


def space(kind, count):
    return [pl.BlockSpec(memory_space=kind)] * count


def shards(conserved, solid_cells, flux_x, flux_y, counts, owner_offset, stencil_base, weights, ghost_cells,
           first_matrix, rest_matrix):
    shape = jax.ShapeDtypeStruct
    gx, gy = lax.axis_index("gx"), lax.axis_index("gy")
    nx, ny = lax.axis_size("gx"), lax.axis_size("gy")
    u = conserved.reshape(F, Z * X, Y)
    vmem, smem, anywhere = pltpu.VMEM, pltpu.SMEM, pl.ANY
    low, high, left, right, info, wide = pl.pallas_call(
        prepare_kernel,
        out_shape=[
            shape((F, HALO * 8, Y), F32), shape((F, HALO * 8, Y), F32),
            shape((F, X, LANES), F32), shape((F, X, LANES), F32),
            shape((9, 8, LANES), I32), shape((4, REC, LANES), F32),
        ],
        in_specs=space(anywhere, 1) + space(smem, 1) + space(vmem, 4),
        out_specs=space(vmem, 6),
        scratch_shapes=[pltpu.VMEM((TILES, F, Z * X, LANES), F32), pltpu.SemaphoreType.DMA((TILES,))],
        compiler_params=pltpu.CompilerParams(vmem_limit_bytes=VMEM_BYTES),
        name="prepare",
    )(u, counts.reshape(1, 1), owner_offset.reshape(1, REC), stencil_base.reshape(1, REC), ghost_cells.reshape(1, REC), weights)
    halos = pl.pallas_call(
        exchange_kernel,
        out_shape=[shape((F, HALO * 8, Y), F32)] * 2 + [shape((F, X, LANES), F32)] * 2
        + [shape((F, 16, LANES), F32)] * 4 + [shape((9, 8, LANES), I32)],
        in_specs=space(vmem, 5),
        out_specs=space(vmem, 9),
        scratch_shapes=[pltpu.SemaphoreType.DMA((16,)), pltpu.SemaphoreType.DMA((16,)), pltpu.SemaphoreType.DMA],
        compiler_params=pltpu.CompilerParams(collective_id=0, has_side_effects=True, vmem_limit_bytes=VMEM_BYTES),
        name="halo",
    )(low, high, left, right, info)
    ghosts = halos[8]
    flags = jnp.stack([gx > 0, gx < nx - 1, gy > 0, gy < ny - 1]).astype(F32)
    section, values = pl.pallas_call(
        main_kernel,
        out_shape=[shape((TILES, F, X * Z, LANES), F32), shape((9, F * Z, LANES), F32)],
        in_specs=space(smem, 4) + space(anywhere, 1) + space(vmem, 9) + space(anywhere, 2) + space(vmem, 1),
        out_specs=space(vmem, 2),
        scratch_shapes=[
            pltpu.VMEM((TILES, F, Z * X, LANES), F32),
            pltpu.VMEM((4, 512, 128), BF16), pltpu.VMEM((4, 768, 256), BF16),
            pltpu.VMEM((TILES, ROWS, LANES), F32), pltpu.VMEM((768, LANES), F32),
        ] + [pltpu.VMEM((TILES + 1, ROWS, LANES), BF16)] * 4 + [
            pltpu.VMEM((2, ROWS, 384), F32),
            pltpu.VMEM((7, F, DROWS, LANES), F32), pltpu.VMEM((F, DROWS, LANES), F32),
            pltpu.SemaphoreType.DMA((12,)),
        ],
        compiler_params=pltpu.CompilerParams(vmem_limit_bytes=VMEM_BYTES),
        name="section",
    )(flags, flux_x * -0.125, flux_y * -0.125, info, u, solid_cells, *halos[:8], first_matrix, rest_matrix, wide)
    arrived = pl.pallas_call(
        record_kernel,
        out_shape=shape((9, F * Z, LANES), F32),
        in_specs=space(vmem, 1),
        out_specs=pl.BlockSpec(memory_space=vmem),
        scratch_shapes=[pltpu.SemaphoreType.DMA((9,)), pltpu.SemaphoreType.DMA((9,)), pltpu.SemaphoreType.DMA],
        compiler_params=pltpu.CompilerParams(collective_id=1, has_side_effects=True, vmem_limit_bytes=VMEM_BYTES),
        name="records",
    )(values)
    sources = [(gx - dx, gy - dy) for dx, dy in OFFSETS]
    valid = jnp.stack([(sx >= 0) & (sx < nx) & (sy >= 0) & (sy < ny) for sx, sy in sources]).astype(F32)
    out = pl.pallas_call(
        scatter_kernel,
        out_shape=shape((F, Z * X, Y), F32),
        in_specs=space(smem, 2) + space(vmem, 2),
        out_specs=pl.BlockSpec(memory_space=anywhere),
        scratch_shapes=[
            pltpu.VMEM((TILES, F, X * Z, LANES), F32), pltpu.VMEM((TILES, F, Z * X, LANES), F32),
            pltpu.SemaphoreType.DMA((TILES,)),
        ],
        compiler_params=pltpu.CompilerParams(vmem_limit_bytes=VMEM_BYTES),
        name="scatter",
    )(valid, ghosts, section, arrived)
    return out.reshape(F, Z, X, Y)


def solution(mesh):
    first, rest = filter_constants()

    def advance(*arguments):
        run = jax.shard_map(
            shards,
            mesh=mesh,
            in_specs=(
                P(None, None, "gx", "gy"), P("gx", "gy"), P(), P(), P(("gx", "gy")), P(("gx", "gy")),
                P(("gx", "gy")), P(("gx", "gy"), None), P(("gx", "gy")), P(), P(),
            ),
            out_specs=P(None, None, "gx", "gy"),
            check_vma=False,
        )
        return run(*arguments, jnp.asarray(first), jnp.asarray(rest))

    return advance
```

profile of v0, /device:TPU:0, one launch (start us, length us, event | category | flops | bytes accessed | tf_op | source)
XLA Modules:
  0.0 107.8 jit_solution(4496683338412842397)
XLA Ops:
  0.7 0.1 stack.54
  0.8 0.6 add_convert_fusion.flags
  1.4 0.6 convert_element_type.6.valid
  1.9 1.3 %reshape.20.code_ref = s32[1,576]{1,0:T(1,128)} reshape(s32[576]{0:T(1024)} %param.16) | data formatting | bytes 4608 | tf_op jit(solution)/shard_map/reshape | solution.py:466
  3.2 1.3 %reshape.21.base_ref = s32[1,576]{1,0:T(1,128)} reshape(s32[576]{0:T(1024)} %param.17) | data formatting | bytes 4608 | tf_op jit(solution)/shard_map/reshape | solution.py:466
  4.5 1.3 %reshape.22.ghost_ref = s32[1,576]{1,0:T(1,128)} reshape(s32[576]{0:T(1024)} %param.19) | data formatting | bytes 4608 | tf_op jit(solution)/shard_map/reshape | solution.py:466
  5.8 1.3 %broadcast_multiply_fusion = (f32[5,5]{1,0:T(8,128)}, f32[5,5]{1,0:T(8,128)}) fusion(f32[5,5]{1,0:T(8,128)} %param.14, f32[5,5]{1,0:T(8,128)} %param.13), kind=kLoop, calls=%fused_computation | loop fusion | flops 50 | bytes 400 | tf_op jit(solution)/shard_map/mul | solution.py:495
  7.1 1.6 %copy.12.weight_ref = f32[576,16]{1,0:T(8,128)} copy(f32[576,16]{0,1:T(8,128)} %param.18) | data formatting | bytes 73728 | tf_op args[7]
  8.7 7.3 %prepare.1 = (f32[5,80,512]{2,1,0:T(8,128)}, f32[5,80,512]{2,1,0:T(8,128)}, f32[5,64,128]{2,1,0:T(8,128)}, f32[5,64,128]{2,1,0:T(8,128)}, s32[9,8,128]{2,1,0:T(8,128)}, /*index=5*/f32[4,576,128]{2,1,0:T(8,128)}) custom-call(f32[5,512,512]{2,1,0:T(8,128)} %bitcast.17, s32[1,1]{1,0:T(1,128)} %bitcast.16.count_ref, s32[1,576]{1,0:T(1,128)} %reshape.20.code_ref, ...), custom_call_target="tpu_custom_call" | custom-call | tf_op jit(solution)/shard_map/prepare/pallas_call | solution.py:454
  16.1 23.3 %halo.1 = (f32[5,80,512]{2,1,0:T(8,128)}, f32[5,80,512]{2,1,0:T(8,128)}, f32[5,64,128]{2,1,0:T(8,128)}, f32[5,64,128]{2,1,0:T(8,128)}, f32[5,16,128]{2,1,0:T(8,1...) custom-call(f32[5,80,512]{2,1,0:T(8,128)} %get-tuple-element.22.low_ref, ...), custom_call_target="tpu_custom_call" | custom-call | tf_op jit(solution)/shard_map/halo/pallas_call | solution.py:467
  39.3 45.0 %section.1 = (f32[4,5,512,128]{3,2,1,0:T(8,128)}, f32[9,40,128]{2,1,0:T(8,128)}) custom-call(f32[4]{0:T(128)} %add_convert_fusion.flags, f32[5,5]{1,0:T(8,128)} %get-tuple-element.40.flux_x, f32[5,5]{1,0:T(8,128)} %get-tuple-element.39.flux_y, s32[9,8,128]{2,1,0:T(8,128)} %get-tuple-element.26.info_ref.info, f32[5,512,512]{2,1,0:T(8,128)} %bitcast.18, ...), custom_call_target="tpu_custom_call" | custom-call | tf_op jit(solution)/shard_map/section/pallas_call | solution.py:479
  84.4 11.0 %records.1.arrived = f32[9,40,128]{2,1,0:T(8,128)} custom-call(f32[9,40,128]{2,1,0:T(8,128)} %get-tuple-element.38.values_ref), custom_call_target="tpu_custom_call" | custom-call | tf_op jit(solution)/shard_map/records/pallas_call | solution.py:496
  95.4 12.4 %scatter.1 = f32[5,512,512]{2,1,0:T(8,128)} custom-call(f32[9]{0:T(128)} %convert_element_type.6.valid, s32[9,8,128]{2,1,0:T(8,128)} %get-tuple-element.27.info, f32[4,5,512,128]{3,2,1,0:T(8,128)} %get-tuple-element.37.section_ref, f32[9,40,128]{2,1,0:T(8,128)} %records.1.arrived), custom_call_target="tpu_custom_call" | custom-call | tf_op jit(solution)/shard_map/scatter/pallas_call | solution.py:507
where the time goes:
time: 109 us; the launch traced here: 108 us
  Pallas kernels  99.1 us (91%)
  local copies, waits for them, and re-layouts  5.57 us (5%)
  other arithmetic  2.48 us (2%)
    pallas_call x1, Pallas kernels, shards(): pl.pallas_call(main_kernel, out_shape=[shape((TILES, F, X * Z, LANES), F3...  45 us
    pallas_call x1, Pallas kernels, shards(): pl.pallas_call(exchange_kernel, out_shape=[shape((F, HALO * 8, Y), F32)]...  23.3 us
    pallas_call x1, Pallas kernels, shards(): pl.pallas_call(scatter_kernel, out_shape=shape((F, Z * X, Y), F32), in_sp...  12.4 us
    pallas_call x1, Pallas kernels, shards(): pl.pallas_call(record_kernel, out_shape=shape((9, F * Z, LANES), F32), in...  11 us
    pallas_call x1, Pallas kernels, shards(): pl.pallas_call(prepare_kernel, out_shape=[shape((F, HALO * 8, Y), F32), s...  7.34 us

commit v1 on v0

v1 whole, which is shorter than its diff:
```python
import functools

import jax
import jax.numpy as jnp
import ml_dtypes
import numpy as np
from jax import lax
from jax.experimental import pallas as pl
from jax.experimental.pallas import tpu as pltpu
from jax.sharding import PartitionSpec as P

F, Z, X, Y = 5, 8, 64, 512
LANES = 128
TILES = Y // LANES
HALO = 10
XE = X + 2 * HALO
ROWS = XE * Z
REC = 576
CAP = 64
SIGNS = (1.0, -1.0, -1.0, -1.0, 1.0)
F32, BF16, I32 = jnp.float32, jnp.bfloat16, jnp.int32
VMEM_BYTES = 60 * 1024 * 1024
OFFSETS = [(k // 3 - 1, k % 3 - 1) for k in range(9)]


def y_matrices(left_edge, right_edge):
    margin = 80
    ys = np.arange(-margin, Y + margin)
    inside = np.ones(ys.shape, bool)
    if left_edge:
        inside &= ys >= 0
    if right_edge:
        inside &= ys < Y
    taps = np.array([1, 6, 15, 20, 15, 6, 1], np.float64) / 64
    single = np.zeros((ys.size, ys.size))
    for offset in range(-3, 4):
        single += np.diag(np.full(ys.size - abs(offset), taps[offset + 3]), offset)
    single = single * inside[:, None] * inside[None, :]
    double = single @ single
    triple = double @ single
    return [-6.0 / 64 * single, 4.0 / 64**2 * double, -1.0 / 64**3 * triple], margin


def block_matrix(powers, margin, y_in, y_out):
    columns = []
    for power in powers:
        full = np.zeros((256, LANES))
        for lane, y in enumerate(y_out):
            if y is not None:
                full[:, lane] = power[y + margin, np.asarray(y_in) + margin]
        columns.append(full)
    return np.concatenate(columns, axis=1)


def filter_constants():
    lane = np.arange(LANES)
    found = []
    for kind in ("mid", "left", "right", "edge_left", "edge_mid", "edge_right"):
        powers, margin = y_matrices(kind.endswith("left"), kind.endswith("right"))
        if kind.startswith("edge"):
            y_in = np.concatenate([np.where(lane < 64, lane, 384 + lane), np.where(lane < 64, Y + lane, lane - 128)])
            y_out = [Y] + [None] * 126 + [-1]
        else:
            c = {"mid": 1, "left": 0, "right": 3}[kind]
            y_in = np.concatenate([128 * c + lane, np.where(lane < 64, 128 * (c + 1) + lane, 128 * (c - 1) + lane)])
            y_out = list(128 * c + lane)
        found.append(block_matrix(powers, margin, np.clip(y_in, -margin, Y + margin - 1), y_out))
    whole = np.stack(found).astype(np.float32)
    high = whole.astype(ml_dtypes.bfloat16)
    low = (whole - high.astype(np.float32)).astype(ml_dtypes.bfloat16)
    first = np.concatenate([high, high], axis=1)[:, :, :128]
    rest = np.concatenate([high, high, low], axis=1)[:, :, 128:]
    return first, rest


def lane_index(rows=8):
    return lax.broadcasted_iota(I32, (rows, LANES), 1)


def prepare_kernel(count_ref, code_ref, base_ref, ghost_ref, weight_ref, info_ref, wide_ref):
    code = code_ref[...].reshape(1, REC)
    base = base_ref[...].reshape(1, REC)
    ghost = ghost_ref[...].reshape(1, REC)
    kinds = lax.broadcasted_iota(I32, (16, REC), 0)
    hits = (kinds == code).astype(F32)
    before = (lax.broadcasted_iota(I32, (REC, REC), 0) < lax.broadcasted_iota(I32, (REC, REC), 1)).astype(F32).astype(BF16)
    ahead = jnp.dot(hits.astype(BF16), before, preferred_element_type=F32)
    rank = jnp.sum(ahead * hits, axis=0, keepdims=True).astype(I32)
    slot = code * CAP + rank
    live = lax.broadcasted_iota(I32, (1, REC), 1) < count_ref[0]
    slot = jnp.where(live, slot, REC)
    placing = (lax.broadcasted_iota(I32, (REC, REC), 0) == slot).astype(F32).astype(BF16)
    base_x = ((base.astype(F32) + 0.5) * (1.0 / (Y - 3))).astype(I32)
    base_y = base - base_x * (Y - 3)
    window = jnp.minimum(base_y // 64, 6)
    first_lane = base_y - window * 64
    ghost_y = ghost % Y
    payload_rows = [window, base_x, ghost // Y, ghost_y // LANES, ghost_y % LANES]
    row_id = lax.broadcasted_iota(I32, (8, REC), 0)
    payload = jnp.zeros((8, REC), I32)
    for row, value in enumerate(payload_rows):
        payload = jnp.where(row_id == row, value, payload)
    payload = payload.astype(F32).astype(BF16)
    across = (((1,), (1,)), ((), ()))
    for k in range(9):
        part = lax.dot_general(payload, placing[k * CAP : (k + 1) * CAP], across, preferred_element_type=F32)
        info_ref[k] = jnp.concatenate([part, jnp.zeros((8, LANES - CAP), F32)], axis=1).astype(I32)
    lanes_hit = (lax.broadcasted_iota(I32, (LANES, REC), 0) == first_lane).astype(F32).astype(BF16)
    starts = lax.dot_general(placing, lanes_hit, across, preferred_element_type=F32)
    weight = weight_ref[...]
    weight_a = weight.astype(BF16)
    left_over = weight - weight_a.astype(F32)
    weight_b = left_over.astype(BF16)
    weight_c = (left_over - weight_b.astype(F32)).astype(BF16)
    ordered = sum(
        lax.dot_general(placing, part, across, preferred_element_type=F32) for part in (weight_a, weight_b, weight_c)
    )
    shifted = [starts] + [pltpu.roll(starts, j, 1) for j in range(1, 4)]
    for i in range(4):
        total = shifted[0] * ordered[:, 4 * i : 4 * i + 1]
        for j in range(1, 4):
            total = total + shifted[j] * ordered[:, 4 * i + j : 4 * i + j + 1]
        wide_ref[i] = total


def neighbour(dx, dy):
    nx, ny = lax.axis_size("gx"), lax.axis_size("gy")
    return (lax.rem(lax.axis_index("gx") + dx + nx, nx), lax.rem(lax.axis_index("gy") + dy + ny, ny))


def signal_neighbours():
    barrier = pltpu.get_barrier_semaphore()
    for dx, dy in OFFSETS:
        if (dx, dy) != (0, 0):
            pl.semaphore_signal(barrier, inc=1, device_id=neighbour(dx, dy), device_id_type=pl.DeviceIdType.MESH)


def wait_neighbours():
    pl.semaphore_wait(pltpu.get_barrier_semaphore(), 8)


class Binomial:
    def __init__(self):
        self.held = [None] * 6

    def push(self, value):
        for i in range(6):
            before, self.held[i] = self.held[i], value
            if before is None:
                return None
            value = before + value
        return value


def remote(source, target, send_sem, recv_sem, offset):
    return pltpu.make_async_remote_copy(
        src_ref=source, dst_ref=target, send_sem=send_sem, recv_sem=recv_sem,
        device_id=neighbour(*offset), device_id_type=pl.DeviceIdType.MESH,
    )


def main_kernel(flux_x, flux_y, info, u_hbm, info_hbm, solid_ref, first_hbm, rest_hbm, wide_ref,
                section_hbm, arrived, ghosts,
                ub, firsts, rests, ut, hs, hi_main, lo_main, hi_side, lo_side, vs, dg, de, section_ref, values_ref,
                low_ref, high_ref, left_ref, right_ref, xlo, xhi, ylo, yhi, cll, clr, chl, chr_,
                sems, row_send, row_recv, side_send, side_recv, record_send, record_recv, out_sems):
    signal_neighbours()
    gx, gy = lax.axis_index("gx"), lax.axis_index("gy")
    last_x, last_y = lax.axis_size("gx") - 1, lax.axis_size("gy") - 1
    flag_lo = jnp.where(gx > 0, 1.0, 0.0).astype(F32)
    flag_hi = jnp.where(gx < last_x, 1.0, 0.0).astype(F32)
    flag_left = jnp.where(gy > 0, 1.0, 0.0).astype(F32)
    flag_right = jnp.where(gy < last_y, 1.0, 0.0).astype(F32)
    kinds = [
        jnp.where(gy == 0, 1, 0),
        0,
        jnp.where(gy == last_y, 2, 0),
        jnp.where(gy == 0, 3, jnp.where(gy == last_y, 5, 4)),
    ]
    copies = [
        pltpu.make_async_copy(u_hbm.at[:, :, pl.ds(c * LANES, LANES)], ub.at[c], sems.at[c]) for c in range(TILES)
    ]
    constant_copies = []
    for i, kind in enumerate(kinds):
        constant_copies.append(pltpu.make_async_copy(first_hbm.at[kind], firsts.at[i], sems.at[4 + i]))
        constant_copies.append(pltpu.make_async_copy(rest_hbm.at[kind], rests.at[i], sems.at[8 + i]))
    for copy in copies + constant_copies:
        copy.start()
    for copy in copies:
        copy.wait()
    lane = lane_index()
    low_half = lane < 64

    def pack_rows(f, carry):
        for c in range(TILES):
            for x in range(HALO):
                low_ref[f, pl.ds(x * 8, 8), pl.ds(c * LANES, LANES)] = ub[c, f, pl.ds(x, 8, stride=X), :]
                high_ref[f, pl.ds(x * 8, 8), pl.ds(c * LANES, LANES)] = ub[c, f, pl.ds(X - HALO + x, 8, stride=X), :]
        return carry

    lax.fori_loop(0, F, pack_rows, 0)
    wait_neighbours()

    def row_copies(f):
        return (
            remote(high_ref.at[f], xlo.at[f], row_send.at[0, f], row_recv.at[0, f], (1, 0)),
            remote(low_ref.at[f], xhi.at[f], row_send.at[1, f], row_recv.at[1, f], (-1, 0)),
        )

    for f in range(F):
        for copy in row_copies(f):
            copy.start()

    def pack_sides(f, carry):
        for octet in range(8):
            left = jnp.zeros((8, LANES), F32)
            right = jnp.zeros((8, LANES), F32)
            for z in range(Z):
                here = (lane // 16) == z
                row = z * X + octet * 8
                left = jnp.where(here, pltpu.roll(ub[0, f, pl.ds(row, 8), :], 16 * z, 1), left)
                right = jnp.where(
                    here, pltpu.roll(ub[TILES - 1, f, pl.ds(row, 8), :], (16 * z - (LANES - HALO)) % LANES, 1), right
                )
            left_ref[f, pl.ds(octet * 8, 8), :] = left
            right_ref[f, pl.ds(octet * 8, 8), :] = right
        return carry

    lax.fori_loop(0, F, pack_sides, 0)
    plan = [
        (right_ref, ylo, (0, 1)),
        (left_ref, yhi, (0, -1)),
        (right_ref.at[:, pl.ds(X - 16, 16)], cll, (1, 1)),
        (left_ref.at[:, pl.ds(X - 16, 16)], clr, (1, -1)),
        (right_ref.at[:, pl.ds(0, 16)], chl, (-1, 1)),
        (left_ref.at[:, pl.ds(0, 16)], chr_, (-1, -1)),
    ]
    for k, offset in enumerate(OFFSETS):
        if k != 4:
            plan.append((info_hbm.at[k], ghosts.at[k], offset))
    side_copies = [
        remote(source, target, side_send.at[index], side_recv.at[index], offset)
        for index, (source, target, offset) in enumerate(plan)
    ]
    for copy in side_copies:
        copy.start()
    own_ghosts = pltpu.make_async_copy(info_hbm.at[4], ghosts.at[4], out_sems.at[0])
    own_ghosts.start()

    def turn(f, carry):
        for c in range(TILES):
            for x in range(X):
                ut[f, c, pl.ds((HALO + x) * 8, 8), :] = ub[c, f, pl.ds(x, 8, stride=X), :]
        return carry

    lax.fori_loop(0, F, turn, 0)
    for copy in constant_copies:
        copy.wait()
    for copy in side_copies:
        copy.wait_recv()

    def per_field(f, carry):
        for copy in row_copies(f):
            copy.wait_recv()
        for c in range(TILES):
            ut[f, c, pl.ds(0, 80), :] = xlo[f, :, pl.ds(c * LANES, LANES)] * flag_lo
            ut[f, c, pl.ds(ROWS - 80, 80), :] = xhi[f, :, pl.ds(c * LANES, LANES)] * flag_hi
        for octet in range(-2, 10):
            if octet < 0:
                left, right = [r[f, pl.ds((octet + 2) * 8, 8), :] * flag_lo for r in (cll, clr)]
            elif octet >= 8:
                left, right = [r[f, pl.ds((octet - 8) * 8, 8), :] * flag_hi for r in (chl, chr_)]
            else:
                left, right = [r[f, pl.ds(octet * 8, 8), :] for r in (ylo, yhi)]
            left, right = left * flag_left, right * flag_right
            for z in range(Z):
                from_right = pltpu.roll(right, (-16 * z) % LANES, 1)
                from_left = pltpu.roll(left, (LANES - HALO - 16 * z) % LANES, 1)
                hs[pl.ds((octet + 2) * 64 + z, 8, stride=8), :] = jnp.where(low_half, from_right, from_left)

        keep_low = (lane_index(16) < 64).astype(F32).astype(BF16)
        keep_high = (lane_index(16) >= 64).astype(F32).astype(BF16)
        for block in range(ROWS // 16):
            rows = pl.ds(block * 16, 16)
            highs, lows = [], []
            for c in range(TILES + 1):
                value = ut[f, c, rows, :] if c < TILES else hs[pl.ds(block * 16 + 48, 16), :]
                high = value.astype(BF16)
                low = (value - high.astype(F32)).astype(BF16)
                highs.append(high)
                lows.append(low)
            for parts, main, side in ((highs, hi_main, hi_side), (lows, lo_main, lo_side)):
                lo_parts = [p * keep_low for p in parts]
                hi_parts = [p * keep_high for p in parts]
                for c in range(TILES):
                    main[c, rows, :] = parts[c]
                    after = lo_parts[c + 1] if c < TILES - 1 else lo_parts[TILES]
                    ahead = hi_parts[c - 1] if c > 0 else hi_parts[TILES]
                    side[c, rows, :] = after + ahead
                main[TILES, rows, :] = lo_parts[0] + hi_parts[TILES - 1]
                side[TILES, rows, :] = parts[TILES]

        for c in range(TILES + 1):
            which = (0, 1, 1, 2, 3)[c]
            high = jnp.concatenate([hi_main[c], hi_side[c]], axis=1)
            low = jnp.concatenate([lo_main[c], lo_side[c]], axis=1)
            vs[c % 2, :, pl.ds(0, 128)] = jnp.dot(
                jnp.concatenate([high, low], axis=1), firsts[which], preferred_element_type=F32
            )
            vs[c % 2, :, pl.ds(128, 256)] = jnp.dot(
                jnp.concatenate([high, low, high], axis=1), rests[which], preferred_element_type=F32
            )
            stages = [Binomial(), Binomial(), Binomial()]

            def mask(value, e):
                return value * flag_lo if e < HALO else value * flag_hi if e >= HALO + X else value

            for e in range(XE):
                value = stages[2].push(vs[c % 2, pl.ds(e * 8, 8), pl.ds(256, 128)])
                if value is None:
                    continue
                value = mask(value, e - 3) + vs[c % 2, pl.ds((e - 3) * 8, 8), pl.ds(128, 128)]
                value = stages[1].push(value)
                if value is None:
                    continue
                value = mask(value, e - 6) + vs[c % 2, pl.ds((e - 6) * 8, 8), pl.ds(0, 128)]
                value = stages[0].push(value)
                if value is None:
                    continue
                at = e - 9
                start = ut[f, c, pl.ds(at * 8, 8), :] if c < TILES else hs[pl.ds(at * 8 + 48, 8), :]
                value = mask(value, at) + 4.0 * start
                if c == TILES:
                    de[f, at - 9] = value
                else:
                    dg[2 * c, f, at - 9] = value
        for x in range(1, X + 1):
            turned = [pltpu.roll(dg[2 * c, f, x], 64, 1) for c in range(TILES)]
            for c in range(TILES - 1):
                dg[2 * c + 1, f, x] = jnp.where(low_half, turned[c], turned[c + 1])
        return carry

    lax.fori_loop(0, F, per_field, 0)

    def record_copy(k):
        offset = (lax.div(k, 3) - 1, lax.rem(k, 3) - 1)
        return remote(values_ref.at[k], arrived.at[k], record_send.at[k], record_recv.at[k], offset)

    def per_code(k, carry):
        def per_group(group, held):
            held = list(held)
            weights = [wide_ref[i, pl.ds(pl.multiple_of(k * CAP + group * 8, 8), 8), :] for i in range(4)]
            for j in range(8):
                slot = group * 8 + j
                window = info[k, 0, slot]
                start = info[k, 1, slot] + 1
                rows = [jnp.broadcast_to(weights[i][j : j + 1, :], (8, LANES)) for i in range(4)]
                for f in range(F):
                    total = dg[window, f, start] * rows[0]
                    for i in range(1, 4):
                        total = total + dg[window, f, start + i] * rows[i]
                    value = jnp.sum(total, axis=1, keepdims=True) * SIGNS[f]
                    held[f] = jnp.where(lane == slot, value, held[f])
            return tuple(held)

        held = lax.fori_loop(0, CAP // 8, per_group, tuple(jnp.zeros((8, LANES), F32) for _ in range(F)))
        for f in range(F):
            values_ref[k, pl.ds(f * 8, 8), :] = held[f]

        @pl.when(k != 4)
        def _():
            record_copy(k).start()

        return carry

    lax.fori_loop(0, 9, per_code, 0)
    own_values = pltpu.make_async_copy(values_ref.at[4], arrived.at[4], out_sems.at[1])
    own_values.start()

    mix_x = [[flux_x[f, g] * -0.125 for g in range(F)] for f in range(F)]
    mix_y = [[flux_y[f, g] * -0.125 for g in range(F)] for f in range(F)]

    def per_octet(octet, carry):
        for c in range(TILES):
            solid = solid_ref[pl.ds(pl.multiple_of(octet * 8, 8), 8), pl.ds(c * LANES, LANES)]
            for half in range(4):
                first = octet * 8 + half * 2
                here = pl.ds(first + 1, 2)
                slopes_x, slopes_y, mids = [], [], []
                wide_lane = lax.broadcasted_iota(I32, (2, 8, LANES), 2)
                for g in range(F):
                    mid = dg[2 * c, g, here]
                    before = dg[2 * c, g, pl.ds(first, 2)]
                    after = dg[2 * c, g, pl.ds(first + 2, 2)]
                    left = dg[2 * (c - 1), g, here] if c > 0 else de[g, here]
                    right = dg[2 * (c + 1), g, here] if c < TILES - 1 else de[g, here]
                    up = jnp.where(wide_lane == LANES - 1, pltpu.roll(right, LANES - 1, 2), pltpu.roll(mid, LANES - 1, 2))
                    down = jnp.where(wide_lane == 0, pltpu.roll(left, 1, 2), pltpu.roll(mid, 1, 2))
                    mids.append(mid)
                    slopes_x.append(after - before)
                    slopes_y.append(up - down)
                for f in range(F):
                    total = -0.125 * mids[f]
                    for g in range(F):
                        total = total + mix_x[f][g] * slopes_x[g] + mix_y[f][g] * slopes_y[g]
                    for i in range(2):
                        x = octet * 8 + half * 2 + i
                        cells = total[i] + 1.125 * ub[c, f, pl.ds(x, 8, stride=X), :]
                        row = half * 2 + i
                        blocked = jnp.broadcast_to(solid[row : row + 1, :], (8, LANES)) == 1
                        section_ref[c, f, pl.ds(pl.multiple_of((first + i) * 8, 8), 8), :] = jnp.where(blocked, 0.0, cells)
        return carry

    written = []
    for half in range(2):
        lax.fori_loop(half * 4, half * 4 + 4, per_octet, 0)
        rows = pl.ds(half * 256, 256)
        written.append(
            pltpu.make_async_copy(section_ref.at[:, :, rows], section_hbm.at[:, :, rows], out_sems.at[2 + half])
        )
        written[-1].start()

    def finish_field(f, carry):
        for copy in row_copies(f):
            copy.wait_send()
        return carry

    lax.fori_loop(0, F, finish_field, 0)
    for copy in side_copies:
        copy.wait_send()
    for k in range(9):
        if k != 4:
            record_copy(k).wait()
    for copy in written + [own_ghosts, own_values]:
        copy.wait()


def scatter_kernel(info, section_hbm, arrived, out_hbm, work, natural, sems):
    loading = pltpu.make_async_copy(section_hbm, work, sems.at[TILES])
    loading.start()
    gx, gy = lax.axis_index("gx"), lax.axis_index("gy")
    nx, ny = lax.axis_size("gx"), lax.axis_size("gy")
    lane = lane_index()
    loading.wait()

    def per_code(k, carry):
        from_x, from_y = gx - lax.div(k, 3) + 1, gy - lax.rem(k, 3) + 1
        weight = jnp.where((from_x >= 0) & (from_x < nx) & (from_y >= 0) & (from_y < ny), 1.0, 0.0).astype(F32)
        blocks = [arrived[k, pl.ds(f * 8, 8), :] * weight for f in range(F)]
        for j in range(CAP):
            start = pl.multiple_of(info[k, 2, j] * 8, 8)
            tile = info[k, 3, j]
            hit = lane == info[k, 4, j]
            for f in range(F):
                value = jnp.broadcast_to(blocks[f][:, j : j + 1], (8, LANES))
                rows = pl.ds(start, 8)
                work[tile, f, rows, :] = work[tile, f, rows, :] + jnp.where(hit, value, 0.0)
        return carry

    lax.fori_loop(0, 9, per_code, 0)
    copies = []
    for c in range(TILES):

        def per_field(f, carry):
            for x in range(X):
                natural[c, f, pl.ds(x, 8, stride=X), :] = work[c, f, pl.ds(x * 8, 8), :]
            return carry

        lax.fori_loop(0, F, per_field, 0)
        copy = pltpu.make_async_copy(natural.at[c], out_hbm.at[:, :, pl.ds(c * LANES, LANES)], sems.at[c])
        copy.start()
        copies.append(copy)
    for copy in copies:
        copy.wait()


def space(kind, count):
    return [pl.BlockSpec(memory_space=kind)] * count


def shards(conserved, solid_cells, flux_x, flux_y, counts, owner_offset, stencil_base, weights, ghost_cells,
           first_matrix, rest_matrix):
    shape = jax.ShapeDtypeStruct
    u = conserved.reshape(F, Z * X, Y)
    vmem, smem, anywhere = pltpu.VMEM, pltpu.SMEM, pl.ANY
    dma = pltpu.SemaphoreType.DMA
    info, wide = pl.pallas_call(
        prepare_kernel,
        out_shape=[shape((9, 8, LANES), I32), shape((4, REC, LANES), F32)],
        in_specs=space(smem, 1) + space(vmem, 4),
        out_specs=space(vmem, 2),
        compiler_params=pltpu.CompilerParams(vmem_limit_bytes=VMEM_BYTES),
        name="prepare",
    )(counts, owner_offset, stencil_base, ghost_cells, weights.T)
    section, arrived, ghosts = pl.pallas_call(
        main_kernel,
        out_shape=[
            shape((TILES, F, X * Z, LANES), F32), shape((9, F * Z, LANES), F32), shape((9, 8, LANES), I32),
        ],
        in_specs=space(smem, 3) + space(anywhere, 2) + space(vmem, 1) + space(anywhere, 2) + space(vmem, 1),
        out_specs=space(anywhere, 3),
        scratch_shapes=[
            pltpu.VMEM((TILES, F, Z * X, LANES), F32),
            pltpu.VMEM((4, 512, 128), BF16), pltpu.VMEM((4, 768, 256), BF16),
            pltpu.VMEM((F, TILES, ROWS, LANES), F32), pltpu.VMEM((768, LANES), F32),
        ] + [pltpu.VMEM((TILES + 1, ROWS, LANES), BF16)] * 4 + [
            pltpu.VMEM((2, ROWS, 384), F32),
            pltpu.VMEM((7, F, X + 2, Z, LANES), F32), pltpu.VMEM((F, X + 2, Z, LANES), F32),
            pltpu.VMEM((TILES, F, X * Z, LANES), F32), pltpu.VMEM((9, F * Z, LANES), F32),
        ] + [pltpu.VMEM((F, HALO * 8, Y), F32)] * 2 + [pltpu.VMEM((F, X, LANES), F32)] * 2
        + [pltpu.VMEM((F, HALO * 8, Y), F32)] * 2 + [pltpu.VMEM((F, X, LANES), F32)] * 2
        + [pltpu.VMEM((F, 16, LANES), F32)] * 4
        + [dma((12,)), dma((2, F)), dma((2, F)), dma((14,)), dma((14,)), dma((9,)), dma((9,)), dma((4,))],
        compiler_params=pltpu.CompilerParams(collective_id=0, has_side_effects=True, vmem_limit_bytes=VMEM_BYTES),
        name="section",
    )(flux_x, flux_y, info, u, info, solid_cells, first_matrix, rest_matrix, wide)
    out = pl.pallas_call(
        scatter_kernel,
        out_shape=shape((F, Z * X, Y), F32),
        in_specs=space(smem, 1) + space(anywhere, 1) + space(vmem, 1),
        out_specs=pl.BlockSpec(memory_space=anywhere),
        scratch_shapes=[
            pltpu.VMEM((TILES, F, X * Z, LANES), F32), pltpu.VMEM((TILES, F, Z * X, LANES), F32), dma((TILES + 1,)),
        ],
        compiler_params=pltpu.CompilerParams(vmem_limit_bytes=VMEM_BYTES),
        name="scatter",
    )(ghosts, section, arrived)
    return out.reshape(F, Z, X, Y)


def solution(mesh):
    first, rest = filter_constants()

    def advance(*arguments):
        run = jax.shard_map(
            shards,
            mesh=mesh,
            in_specs=(
                P(None, None, "gx", "gy"), P("gx", "gy"), P(), P(), P(("gx", "gy")), P(("gx", "gy")),
                P(("gx", "gy")), P(("gx", "gy"), None), P(("gx", "gy")), P(), P(),
            ),
            out_specs=P(None, None, "gx", "gy"),
            check_vma=False,
        )
        return run(*arguments, jnp.asarray(first), jnp.asarray(rest))

    return advance
```

time: 109 us -> 81.4 us (0.75)
  Pallas kernels: 99.1 us -> 80.5 us
  local copies, waits for them, and re-layouts: 5.57 us -> 0 us
  other arithmetic: 2.48 us -> 0 us
    pallas_call x3 -> x1, Pallas kernels: 41.7 us -> 4.72 us  [shards(): pl.pallas_call(prepare_kernel, out_shape=[shape((9, 8, LANES), I32), shap...]
    pallas_call x1, Pallas kernels: 45 us -> 62.3 us  [shards(): pl.pallas_call(main_kernel, out_shape=[shape((TILES, F, X * Z, LANES), F3...]
    reshape x3 -> x0, local copies, waits for them, and re-layouts: 3.82 us -> none  [the longest x1 1.28 us: shards(): owner_offset.reshape(1, REC)]
    unnamed x1 -> x0, local copies, waits for them, and re-layouts: 1.64 us -> none
    mul x1 -> x0, other arithmetic: 1.3 us -> none  [shards(): flux_y * -0.125]
    convert_element_type x2 -> x0, other arithmetic: 1.18 us -> none  [the longest x1 0.6 us: shards(): flags = jnp.stack([gx > 0, gx < nx - 1, gy > 0, gy < ny - 1]).astype(F32)]
where the time goes in v1:
time: 81.4 us; the launch traced here: 81.1 us
  Pallas kernels  80.5 us (99%)
    pallas_call x1, Pallas kernels, shards(): pl.pallas_call(main_kernel, out_shape=[shape((TILES, F, X * Z, LANES), F3...  62.3 us
    pallas_call x1, Pallas kernels, shards(): pl.pallas_call(scatter_kernel, out_shape=shape((F, Z * X, Y), F32), in_sp...  13.4 us
    pallas_call x1, Pallas kernels, shards(): pl.pallas_call(prepare_kernel, out_shape=[shape((9, 8, LANES), I32), shap...  4.72 us

profile of v1, /device:TPU:0, one launch (start us, length us, event | category | flops | bytes accessed | tf_op | source)
XLA Modules:
  0.0 81.1 jit_solution(3600702442072807720)
XLA Ops:
  0.7 4.7 %prepare.1 = (s32[9,8,128]{2,1,0:T(8,128)}, f32[4,576,128]{2,1,0:T(8,128)}) custom-call(s32[1]{0:T(128)S(6)} %copy.12.count_ref, s32[576]{0:T(1024)} %code_ref.1, s32[576]{0:T(1024)} %base_ref.1, s32[576]{0:T(1024)} %ghost_ref.1, f32[16,576]{1,0:T(8,128)} %bitcast.4), custom_call_target="tpu_custom_call" | custom-call | tf_op jit(solution)/shard_map/prepare/pallas_call | solution.py:487
  5.4 62.3 %section.1 = (f32[4,5,512,128]{3,2,1,0:T(8,128)}, f32[9,40,128]{2,1,0:T(8,128)}, s32[9,8,128]{2,1,0:T(8,128)}) custom-call(f32[5,5]{1,0:T(8,128)} %flux_x.1, f32[5,5]{1,0:T(8,128)} %flux_y.1, s32[9,8,128]{2,1,0:T(8,128)} %get-tuple-element.10.info.info_hbm, f32[5,512,512]{2,1,0:T(8,128)} %bitcast.3, s32[9,8,128]{2,1,0:T(8,128)} %get-tuple-element.10.info.info_hbm, ...), custom_call_target="tpu_custom_call" | custom-call | tf_op jit(solution)/shard_map/section/pallas_call | solution.py:495
  67.7 13.4 %scatter.1 = f32[5,512,512]{2,1,0:T(8,128)} custom-call(s32[9,8,128]{2,1,0:T(8,128)} %get-tuple-element.12.info, f32[4,5,512,128]{3,2,1,0:T(8,128)} %get-tuple-element.13.section_hbm, f32[9,40,128]{2,1,0:T(8,128)} %get-tuple-element.14.arrived), custom_call_target="tpu_custom_call" | custom-call | tf_op jit(solution)/shard_map/scatter/pallas_call | solution.py:517

commit v2 on v1

--- a/solution.py
+++ b/solution.py
@@ -77,10 +77,12 @@
     return lax.broadcasted_iota(I32, (rows, LANES), 1)
 
 
-def prepare_kernel(count_ref, code_ref, base_ref, ghost_ref, weight_ref, info_ref, wide_ref):
+ACROSS = (((1,), (1,)), ((), ()))
+
+
+def place_records(count_ref, code_ref, base_ref):
     code = code_ref[...].reshape(1, REC)
     base = base_ref[...].reshape(1, REC)
-    ghost = ghost_ref[...].reshape(1, REC)
     kinds = lax.broadcasted_iota(I32, (16, REC), 0)
     hits = (kinds == code).astype(F32)
     before = (lax.broadcasted_iota(I32, (REC, REC), 0) < lax.broadcasted_iota(I32, (REC, REC), 1)).astype(F32).astype(BF16)
@@ -93,7 +95,12 @@
     base_x = ((base.astype(F32) + 0.5) * (1.0 / (Y - 3))).astype(I32)
     base_y = base - base_x * (Y - 3)
     window = jnp.minimum(base_y // 64, 6)
-    first_lane = base_y - window * 64
+    return placing, window, base_x, base_y - window * 64
+
+
+def prepare_kernel(count_ref, code_ref, base_ref, ghost_ref, info_ref):
+    placing, window, base_x, _ = place_records(count_ref, code_ref, base_ref)
+    ghost = ghost_ref[...].reshape(1, REC)
     ghost_y = ghost % Y
     payload_rows = [window, base_x, ghost // Y, ghost_y // LANES, ghost_y % LANES]
     row_id = lax.broadcasted_iota(I32, (8, REC), 0)
@@ -101,19 +108,22 @@
     for row, value in enumerate(payload_rows):
         payload = jnp.where(row_id == row, value, payload)
     payload = payload.astype(F32).astype(BF16)
-    across = (((1,), (1,)), ((), ()))
     for k in range(9):
-        part = lax.dot_general(payload, placing[k * CAP : (k + 1) * CAP], across, preferred_element_type=F32)
+        part = lax.dot_general(payload, placing[k * CAP : (k + 1) * CAP], ACROSS, preferred_element_type=F32)
         info_ref[k] = jnp.concatenate([part, jnp.zeros((8, LANES - CAP), F32)], axis=1).astype(I32)
+
+
+def spread_weights(count_ref, code_ref, base_ref, weight_ref, wide_ref):
+    placing, _, _, first_lane = place_records(count_ref, code_ref, base_ref)
     lanes_hit = (lax.broadcasted_iota(I32, (LANES, REC), 0) == first_lane).astype(F32).astype(BF16)
-    starts = lax.dot_general(placing, lanes_hit, across, preferred_element_type=F32)
+    starts = lax.dot_general(placing, lanes_hit, ACROSS, preferred_element_type=F32)
     weight = weight_ref[...]
     weight_a = weight.astype(BF16)
     left_over = weight - weight_a.astype(F32)
     weight_b = left_over.astype(BF16)
     weight_c = (left_over - weight_b.astype(F32)).astype(BF16)
     ordered = sum(
-        lax.dot_general(placing, part, across, preferred_element_type=F32) for part in (weight_a, weight_b, weight_c)
+        lax.dot_general(placing, part, ACROSS, preferred_element_type=F32) for part in (weight_a, weight_b, weight_c)
     )
     shifted = [starts] + [pltpu.roll(starts, j, 1) for j in range(1, 4)]
     for i in range(4):
@@ -159,11 +169,11 @@
     )
 
 
-def main_kernel(flux_x, flux_y, info, u_hbm, info_hbm, solid_ref, first_hbm, rest_hbm, wide_ref,
+def main_kernel(flux_x, flux_y, count_ref, info, u_hbm, info_hbm, code_ref, base_ref, weight_ref, solid_ref, first_hbm, rest_hbm,
                 section_hbm, arrived, ghosts,
                 ub, firsts, rests, ut, hs, hi_main, lo_main, hi_side, lo_side, vs, dg, de, section_ref, values_ref,
                 low_ref, high_ref, left_ref, right_ref, xlo, xhi, ylo, yhi, cll, clr, chl, chr_,
-                sems, row_send, row_recv, side_send, side_recv, record_send, record_recv, out_sems):
+                wide_ref, sems, row_send, row_recv, side_send, side_recv, record_send, record_recv, out_sems):
     signal_neighbours()
     gx, gy = lax.axis_index("gx"), lax.axis_index("gy")
     last_x, last_y = lax.axis_size("gx") - 1, lax.axis_size("gy") - 1
@@ -191,26 +201,6 @@
     lane = lane_index()
     low_half = lane < 64
 
-    def pack_rows(f, carry):
-        for c in range(TILES):
-            for x in range(HALO):
-                low_ref[f, pl.ds(x * 8, 8), pl.ds(c * LANES, LANES)] = ub[c, f, pl.ds(x, 8, stride=X), :]
-                high_ref[f, pl.ds(x * 8, 8), pl.ds(c * LANES, LANES)] = ub[c, f, pl.ds(X - HALO + x, 8, stride=X), :]
-        return carry
-
-    lax.fori_loop(0, F, pack_rows, 0)
-    wait_neighbours()
-
-    def row_copies(f):
-        return (
-            remote(high_ref.at[f], xlo.at[f], row_send.at[0, f], row_recv.at[0, f], (1, 0)),
-            remote(low_ref.at[f], xhi.at[f], row_send.at[1, f], row_recv.at[1, f], (-1, 0)),
-        )
-
-    for f in range(F):
-        for copy in row_copies(f):
-            copy.start()
-
     def pack_sides(f, carry):
         for octet in range(8):
             left = jnp.zeros((8, LANES), F32)
@@ -227,6 +217,7 @@
         return carry
 
     lax.fori_loop(0, F, pack_sides, 0)
+    wait_neighbours()
     plan = [
         (right_ref, ylo, (0, 1)),
         (left_ref, yhi, (0, -1)),
@@ -235,14 +226,37 @@
         (right_ref.at[:, pl.ds(0, 16)], chl, (-1, 1)),
         (left_ref.at[:, pl.ds(0, 16)], chr_, (-1, -1)),
     ]
-    for k, offset in enumerate(OFFSETS):
-        if k != 4:
-            plan.append((info_hbm.at[k], ghosts.at[k], offset))
     side_copies = [
         remote(source, target, side_send.at[index], side_recv.at[index], offset)
         for index, (source, target, offset) in enumerate(plan)
     ]
     for copy in side_copies:
+        copy.start()
+
+    def pack_rows(f, carry):
+        for c in range(TILES):
+            for x in range(HALO):
+                low_ref[f, pl.ds(x * 8, 8), pl.ds(c * LANES, LANES)] = ub[c, f, pl.ds(x, 8, stride=X), :]
+                high_ref[f, pl.ds(x * 8, 8), pl.ds(c * LANES, LANES)] = ub[c, f, pl.ds(X - HALO + x, 8, stride=X), :]
+        return carry
+
+    lax.fori_loop(0, F, pack_rows, 0)
+    def row_copies(f):
+        return (
+            remote(high_ref.at[f], xlo.at[f], row_send.at[0, f], row_recv.at[0, f], (1, 0)),
+            remote(low_ref.at[f], xhi.at[f], row_send.at[1, f], row_recv.at[1, f], (-1, 0)),
+        )
+
+    for f in range(F):
+        for copy in row_copies(f):
+            copy.start()
+
+    spread_weights(count_ref, code_ref, base_ref, weight_ref, wide_ref)
+    ghost_copies = [
+        remote(info_hbm.at[k], ghosts.at[k], side_send.at[6 + k], side_recv.at[6 + k], offset)
+        for k, offset in enumerate(OFFSETS) if k != 4
+    ]
+    for copy in ghost_copies:
         copy.start()
     own_ghosts = pltpu.make_async_copy(info_hbm.at[4], ghosts.at[4], out_sems.at[0])
     own_ghosts.start()
@@ -347,8 +361,8 @@
         return remote(values_ref.at[k], arrived.at[k], record_send.at[k], record_recv.at[k], offset)
 
     def per_code(k, carry):
-        def per_group(group, held):
-            held = list(held)
+        held = [jnp.zeros((8, LANES), F32) for _ in range(F)]
+        for group in range(CAP // 8):
             weights = [wide_ref[i, pl.ds(pl.multiple_of(k * CAP + group * 8, 8), 8), :] for i in range(4)]
             for j in range(8):
                 slot = group * 8 + j
@@ -361,9 +375,6 @@
                         total = total + dg[window, f, start + i] * rows[i]
                     value = jnp.sum(total, axis=1, keepdims=True) * SIGNS[f]
                     held[f] = jnp.where(lane == slot, value, held[f])
-            return tuple(held)
-
-        held = lax.fori_loop(0, CAP // 8, per_group, tuple(jnp.zeros((8, LANES), F32) for _ in range(F)))
         for f in range(F):
             values_ref[k, pl.ds(f * 8, 8), :] = held[f]
 
@@ -405,7 +416,7 @@
                         total = total + mix_x[f][g] * slopes_x[g] + mix_y[f][g] * slopes_y[g]
                     for i in range(2):
                         x = octet * 8 + half * 2 + i
-                        cells = total[i] + 1.125 * ub[c, f, pl.ds(x, 8, stride=X), :]
+                        cells = total[i] + 1.125 * ut[f, c, pl.ds(pl.multiple_of((x + HALO) * 8, 8), 8), :]
                         row = half * 2 + i
                         blocked = jnp.broadcast_to(solid[row : row + 1, :], (8, LANES)) == 1
                         section_ref[c, f, pl.ds(pl.multiple_of((first + i) * 8, 8), 8), :] = jnp.where(blocked, 0.0, cells)
@@ -428,6 +439,8 @@
     lax.fori_loop(0, F, finish_field, 0)
     for copy in side_copies:
         copy.wait_send()
+    for copy in ghost_copies:
+        copy.wait()
     for k in range(9):
         if k != 4:
             record_copy(k).wait()
@@ -435,13 +448,20 @@
         copy.wait()
 
 
-def scatter_kernel(info, section_hbm, arrived, out_hbm, work, natural, sems):
-    loading = pltpu.make_async_copy(section_hbm, work, sems.at[TILES])
+def scatter_kernel(info, section_hbm, arrived, out_hbm, section_ref, work, natural, sems):
+    loading = pltpu.make_async_copy(section_hbm, section_ref, sems.at[TILES])
     loading.start()
     gx, gy = lax.axis_index("gx"), lax.axis_index("gy")
     nx, ny = lax.axis_size("gx"), lax.axis_size("gy")
     lane = lane_index()
-    loading.wait()
+
+    def clear(f, carry):
+        for c in range(TILES):
+            for x in range(X):
+                work[c, f, pl.ds(x * 8, 8), :] = jnp.zeros((8, LANES), F32)
+        return carry
+
+    lax.fori_loop(0, F, clear, 0)
 
     def per_code(k, carry):
         from_x, from_y = gx - lax.div(k, 3) + 1, gy - lax.rem(k, 3) + 1
@@ -451,19 +471,24 @@
             start = pl.multiple_of(info[k, 2, j] * 8, 8)
             tile = info[k, 3, j]
             hit = lane == info[k, 4, j]
+            rows = pl.ds(start, 8)
+            held = [work[tile, f, rows, :] for f in range(F)]
             for f in range(F):
                 value = jnp.broadcast_to(blocks[f][:, j : j + 1], (8, LANES))
-                rows = pl.ds(start, 8)
-                work[tile, f, rows, :] = work[tile, f, rows, :] + jnp.where(hit, value, 0.0)
+                held[f] = held[f] + jnp.where(hit, value, 0.0)
+            for f in range(F):
+                work[tile, f, rows, :] = held[f]
         return carry
 
     lax.fori_loop(0, 9, per_code, 0)
+    loading.wait()
     copies = []
     for c in range(TILES):
 
         def per_field(f, carry):
             for x in range(X):
-                natural[c, f, pl.ds(x, 8, stride=X), :] = work[c, f, pl.ds(x * 8, 8), :]
+                rows = pl.ds(x * 8, 8)
+                natural[c, f, pl.ds(x, 8, stride=X), :] = section_ref[c, f, rows, :] + work[c, f, rows, :]
             return carry
 
         lax.fori_loop(0, F, per_field, 0)
@@ -484,20 +509,20 @@
     u = conserved.reshape(F, Z * X, Y)
     vmem, smem, anywhere = pltpu.VMEM, pltpu.SMEM, pl.ANY
     dma = pltpu.SemaphoreType.DMA
-    info, wide = pl.pallas_call(
+    info = pl.pallas_call(
         prepare_kernel,
-        out_shape=[shape((9, 8, LANES), I32), shape((4, REC, LANES), F32)],
-        in_specs=space(smem, 1) + space(vmem, 4),
-        out_specs=space(vmem, 2),
+        out_shape=shape((9, 8, LANES), I32),
+        in_specs=space(smem, 1) + space(vmem, 3),
+        out_specs=pl.BlockSpec(memory_space=vmem),
         compiler_params=pltpu.CompilerParams(vmem_limit_bytes=VMEM_BYTES),
         name="prepare",
-    )(counts, owner_offset, stencil_base, ghost_cells, weights.T)
+    )(counts, owner_offset, stencil_base, ghost_cells)
     section, arrived, ghosts = pl.pallas_call(
         main_kernel,
         out_shape=[
             shape((TILES, F, X * Z, LANES), F32), shape((9, F * Z, LANES), F32), shape((9, 8, LANES), I32),
         ],
-        in_specs=space(smem, 3) + space(anywhere, 2) + space(vmem, 1) + space(anywhere, 2) + space(vmem, 1),
+        in_specs=space(smem, 4) + space(anywhere, 2) + space(vmem, 4) + space(anywhere, 2),
         out_specs=space(anywhere, 3),
         scratch_shapes=[
             pltpu.VMEM((TILES, F, Z * X, LANES), F32),
@@ -510,17 +535,21 @@
         ] + [pltpu.VMEM((F, HALO * 8, Y), F32)] * 2 + [pltpu.VMEM((F, X, LANES), F32)] * 2
         + [pltpu.VMEM((F, HALO * 8, Y), F32)] * 2 + [pltpu.VMEM((F, X, LANES), F32)] * 2
         + [pltpu.VMEM((F, 16, LANES), F32)] * 4
-        + [dma((12,)), dma((2, F)), dma((2, F)), dma((14,)), dma((14,)), dma((9,)), dma((9,)), dma((4,))],
+        + [pltpu.VMEM((4, REC, LANES), F32)]
+        + [dma((12,)), dma((2, F)), dma((2, F)), dma((15,)), dma((15,)), dma((9,)), dma((9,)), dma((4,))],
         compiler_params=pltpu.CompilerParams(collective_id=0, has_side_effects=True, vmem_limit_bytes=VMEM_BYTES),
         name="section",
-    )(flux_x, flux_y, info, u, info, solid_cells, first_matrix, rest_matrix, wide)
+    )(
+        flux_x, flux_y, counts, info, u, info, owner_offset, stencil_base, weights.T, solid_cells, first_matrix, rest_matrix
+    )
     out = pl.pallas_call(
         scatter_kernel,
         out_shape=shape((F, Z * X, Y), F32),
         in_specs=space(smem, 1) + space(anywhere, 1) + space(vmem, 1),
         out_specs=pl.BlockSpec(memory_space=anywhere),
         scratch_shapes=[
-            pltpu.VMEM((TILES, F, X * Z, LANES), F32), pltpu.VMEM((TILES, F, Z * X, LANES), F32), dma((TILES + 1,)),
+            pltpu.VMEM((TILES, F, X * Z, LANES), F32), pltpu.VMEM((TILES, F, X * Z, LANES), F32),
+            pltpu.VMEM((TILES, F, Z * X, LANES), F32), dma((TILES + 1,)),
         ],
         compiler_params=pltpu.CompilerParams(vmem_limit_bytes=VMEM_BYTES),
         name="scatter",

time: 81.4 us -> 61.2 us (0.75)
  Pallas kernels: 80.5 us -> 60.3 us
    pallas_call x1, Pallas kernels: 62.3 us -> 47 us  [shards(): pl.pallas_call(main_kernel, out_shape=[shape((TILES, F, X * Z, LANES), F3...]
    pallas_call x1, Pallas kernels: 4.72 us -> 1.94 us  [shards(): pl.pallas_call(prepare_kernel, out_shape=shape((9, 8, LANES), I32), in_sp...]
    pallas_call x1, Pallas kernels: 13.4 us -> 11.3 us  [shards(): pl.pallas_call(scatter_kernel, out_shape=shape((F, Z * X, Y), F32), in_sp...]
where the time goes in v2:
time: 61.2 us; the launch traced here: 61 us
  Pallas kernels  60.3 us (99%)
  between operations  0.66 us (1%)
    pallas_call x1, Pallas kernels, shards(): pl.pallas_call(main_kernel, out_shape=[shape((TILES, F, X * Z, LANES), F3...  47 us
    pallas_call x1, Pallas kernels, shards(): pl.pallas_call(scatter_kernel, out_shape=shape((F, Z * X, Y), F32), in_sp...  11.3 us
    pallas_call x1, Pallas kernels, shards(): pl.pallas_call(prepare_kernel, out_shape=shape((9, 8, LANES), I32), in_sp...  1.94 us

profile of v2, /device:TPU:0, one launch (start us, length us, event | category | flops | bytes accessed | tf_op | source)
XLA Modules:
  0.0 61.0 jit_solution(5284447283437659001)
XLA Ops:
  0.7 1.9 %prepare.1.info.info_hbm = s32[9,8,128]{2,1,0:T(8,128)} custom-call(s32[1]{0:T(128)S(6)} %copy.12.count_ref, s32[576]{0:T(1024)} %code_ref.3, s32[576]{0:T(1024)} %base_ref.3, s32[576]{0:T(1024)} %ghost_ref.1), custom_call_target="tpu_custom_call" | custom-call | tf_op jit(solution)/shard_map/prepare/pallas_call | solution.py:512
  2.6 47.0 %section.1 = (f32[4,5,512,128]{3,2,1,0:T(8,128)}, f32[9,40,128]{2,1,0:T(8,128)}, s32[9,8,128]{2,1,0:T(8,128)}) custom-call(f32[5,5]{1,0:T(8,128)} %flux_x.1, f32[5,5]{1,0:T(8,128)} %flux_y.1, s32[1]{0:T(128)S(6)} %copy.12.count_ref, s32[9,8,128]{2,1,0:T(8,128)} %prepare.1.info.info_hbm, f32[5,512,512]{2,1,0:T(8,128)} %bitcast.3, ...), custom_call_target="tpu_custom_call" | custom-call | tf_op jit(solution)/shard_map/section/pallas_call | solution.py:520
  49.6 11.3 %scatter.1 = f32[5,512,512]{2,1,0:T(8,128)} custom-call(s32[9,8,128]{2,1,0:T(8,128)} %get-tuple-element.8.info, f32[4,5,512,128]{3,2,1,0:T(8,128)} %get-tuple-element.9.section_hbm, f32[9,40,128]{2,1,0:T(8,128)} %get-tuple-element.10.arrived), custom_call_target="tpu_custom_call" | custom-call | tf_op jit(solution)/shard_map/scatter/pallas_call | solution.py:545

commit v3 on v2

--- a/solution.py
+++ b/solution.py
@@ -13,6 +13,7 @@
 LANES = 128
 TILES = Y // LANES
 HALO = 10
+EDGE = 24
 XE = X + 2 * HALO
 ROWS = XE * Z
 REC = 576
@@ -64,7 +65,11 @@
             c = {"mid": 1, "left": 0, "right": 3}[kind]
             y_in = np.concatenate([128 * c + lane, np.where(lane < 64, 128 * (c + 1) + lane, 128 * (c - 1) + lane)])
             y_out = list(128 * c + lane)
-        found.append(block_matrix(powers, margin, np.clip(y_in, -margin, Y + margin - 1), y_out))
+        block = block_matrix(powers, margin, np.clip(y_in, -margin, Y + margin - 1), y_out)
+        if kind.startswith("edge"):
+            apart = block.reshape(2, LANES, 3, LANES)
+            block = sum(np.roll(apart, (EDGE * f, EDGE * f), (1, 3)) for f in range(F)).reshape(256, 3 * LANES)
+        found.append(block)
     whole = np.stack(found).astype(np.float32)
     high = whole.astype(ml_dtypes.bfloat16)
     low = (whole - high.astype(np.float32)).astype(ml_dtypes.bfloat16)
@@ -171,7 +176,7 @@
 
 def main_kernel(flux_x, flux_y, count_ref, info, u_hbm, info_hbm, code_ref, base_ref, weight_ref, solid_ref, first_hbm, rest_hbm,
                 section_hbm, arrived, ghosts,
-                ub, firsts, rests, ut, hs, hi_main, lo_main, hi_side, lo_side, vs, dg, de, section_ref, values_ref,
+                ub, firsts, rests, ut, hs, edge_in, edge_out, hi_main, lo_main, hi_side, lo_side, vs, dg, de, section_ref, values_ref,
                 low_ref, high_ref, left_ref, right_ref, xlo, xhi, ylo, yhi, cll, clr, chl, chr_,
                 wide_ref, sems, row_send, row_recv, side_send, side_recv, record_send, record_recv, out_sems):
     signal_neighbours()
@@ -273,6 +278,48 @@
     for copy in side_copies:
         copy.wait_recv()
 
+    def filter_block(c, which, f):
+        high = jnp.concatenate([hi_main[c], hi_side[c]], axis=1)
+        low = jnp.concatenate([lo_main[c], lo_side[c]], axis=1)
+        vs[c % 2, :, pl.ds(0, 128)] = jnp.dot(
+            jnp.concatenate([high, low], axis=1), firsts[which], preferred_element_type=F32
+        )
+        vs[c % 2, :, pl.ds(128, 256)] = jnp.dot(
+            jnp.concatenate([high, low, high], axis=1), rests[which], preferred_element_type=F32
+        )
+        stages = [Binomial(), Binomial(), Binomial()]
+
+        def mask(value, e):
+            return value * flag_lo if e < HALO else value * flag_hi if e >= HALO + X else value
+
+        for e in range(XE):
+            value = stages[2].push(vs[c % 2, pl.ds(e * 8, 8), pl.ds(256, 128)])
+            if value is None:
+                continue
+            value = mask(value, e - 3) + vs[c % 2, pl.ds((e - 3) * 8, 8), pl.ds(128, 128)]
+            value = stages[1].push(value)
+            if value is None:
+                continue
+            value = mask(value, e - 6) + vs[c % 2, pl.ds((e - 6) * 8, 8), pl.ds(0, 128)]
+            value = stages[0].push(value)
+            if value is None:
+                continue
+            at = e - 9
+            start = ut[f, c, pl.ds(at * 8, 8), :] if c < TILES else edge_out[pl.ds(at * 8, 8), :]
+            value = mask(value, at) + 4.0 * start
+            if c == TILES:
+                de[at - 9] = value
+            else:
+                dg[2 * c, f, at - 9] = value
+
+    def clear_edges(e, carry):
+        rows = pl.ds(pl.multiple_of(e * 8, 8), 8)
+        edge_in[rows, :] = jnp.zeros((8, LANES), F32)
+        edge_out[rows, :] = jnp.zeros((8, LANES), F32)
+        return carry
+
+    lax.fori_loop(0, XE, clear_edges, 0)
+
     def per_field(f, carry):
         for copy in row_copies(f):
             copy.wait_recv()
@@ -291,6 +338,14 @@
                 from_right = pltpu.roll(right, (-16 * z) % LANES, 1)
                 from_left = pltpu.roll(left, (LANES - HALO - 16 * z) % LANES, 1)
                 hs[pl.ds((octet + 2) * 64 + z, 8, stride=8), :] = jnp.where(low_half, from_right, from_left)
+
+        window = ((lane - EDGE * f + EDGE // 2) & (LANES - 1)) < EDGE
+        for e in range(XE):
+            rows = pl.ds(e * 8, 8)
+            inner = jnp.where(low_half, ut[f, 0, rows, :], ut[f, TILES - 1, rows, :])
+            edge_in[rows, :] = jnp.where(window, pltpu.roll(inner, EDGE * f, 1), edge_in[rows, :])
+            outer = hs[pl.ds(e * 8 + 48, 8), :]
+            edge_out[rows, :] = jnp.where(window, pltpu.roll(outer, EDGE * f, 1), edge_out[rows, :])
 
         keep_low = (lane_index(16) < 64).astype(F32).astype(BF16)
         keep_high = (lane_index(16) >= 64).astype(F32).astype(BF16)
@@ -311,43 +366,9 @@
                     after = lo_parts[c + 1] if c < TILES - 1 else lo_parts[TILES]
                     ahead = hi_parts[c - 1] if c > 0 else hi_parts[TILES]
                     side[c, rows, :] = after + ahead
-                main[TILES, rows, :] = lo_parts[0] + hi_parts[TILES - 1]
-                side[TILES, rows, :] = parts[TILES]
-
-        for c in range(TILES + 1):
-            which = (0, 1, 1, 2, 3)[c]
-            high = jnp.concatenate([hi_main[c], hi_side[c]], axis=1)
-            low = jnp.concatenate([lo_main[c], lo_side[c]], axis=1)
-            vs[c % 2, :, pl.ds(0, 128)] = jnp.dot(
-                jnp.concatenate([high, low], axis=1), firsts[which], preferred_element_type=F32
-            )
-            vs[c % 2, :, pl.ds(128, 256)] = jnp.dot(
-                jnp.concatenate([high, low, high], axis=1), rests[which], preferred_element_type=F32
-            )
-            stages = [Binomial(), Binomial(), Binomial()]
-
-            def mask(value, e):
-                return value * flag_lo if e < HALO else value * flag_hi if e >= HALO + X else value
-
-            for e in range(XE):
-                value = stages[2].push(vs[c % 2, pl.ds(e * 8, 8), pl.ds(256, 128)])
-                if value is None:
-                    continue
-                value = mask(value, e - 3) + vs[c % 2, pl.ds((e - 3) * 8, 8), pl.ds(128, 128)]
-                value = stages[1].push(value)
-                if value is None:
-                    continue
-                value = mask(value, e - 6) + vs[c % 2, pl.ds((e - 6) * 8, 8), pl.ds(0, 128)]
-                value = stages[0].push(value)
-                if value is None:
-                    continue
-                at = e - 9
-                start = ut[f, c, pl.ds(at * 8, 8), :] if c < TILES else hs[pl.ds(at * 8 + 48, 8), :]
-                value = mask(value, at) + 4.0 * start
-                if c == TILES:
-                    de[f, at - 9] = value
-                else:
-                    dg[2 * c, f, at - 9] = value
+
+        for c in range(TILES):
+            filter_block(c, (0, 1, 1, 2)[c], f)
         for x in range(1, X + 1):
             turned = [pltpu.roll(dg[2 * c, f, x], 64, 1) for c in range(TILES)]
             for c in range(TILES - 1):
@@ -355,6 +376,13 @@
         return carry
 
     lax.fori_loop(0, F, per_field, 0)
+    for block in range(ROWS // 16):
+        rows = pl.ds(block * 16, 16)
+        for source, high_ref_, low_ref_ in ((edge_in, hi_main, lo_main), (edge_out, hi_side, lo_side)):
+            high = source[rows, :].astype(BF16)
+            high_ref_[TILES, rows, :] = high
+            low_ref_[TILES, rows, :] = (source[rows, :] - high.astype(F32)).astype(BF16)
+    filter_block(TILES, 3, 0)
 
     def record_copy(k):
         offset = (lax.div(k, 3) - 1, lax.rem(k, 3) - 1)
@@ -403,10 +431,12 @@
                     mid = dg[2 * c, g, here]
                     before = dg[2 * c, g, pl.ds(first, 2)]
                     after = dg[2 * c, g, pl.ds(first + 2, 2)]
-                    left = dg[2 * (c - 1), g, here] if c > 0 else de[g, here]
-                    right = dg[2 * (c + 1), g, here] if c < TILES - 1 else de[g, here]
-                    up = jnp.where(wide_lane == LANES - 1, pltpu.roll(right, LANES - 1, 2), pltpu.roll(mid, LANES - 1, 2))
-                    down = jnp.where(wide_lane == 0, pltpu.roll(left, 1, 2), pltpu.roll(mid, 1, 2))
+                    left = dg[2 * (c - 1), g, here] if c > 0 else de[here]
+                    right = dg[2 * (c + 1), g, here] if c < TILES - 1 else de[here]
+                    left_turn = 1 if c > 0 else (1 - EDGE * g) % LANES
+                    right_turn = LANES - 1 if c < TILES - 1 else (LANES - 1 - EDGE * g) % LANES
+                    up = jnp.where(wide_lane == LANES - 1, pltpu.roll(right, right_turn, 2), pltpu.roll(mid, LANES - 1, 2))
+                    down = jnp.where(wide_lane == 0, pltpu.roll(left, left_turn, 2), pltpu.roll(mid, 1, 2))
                     mids.append(mid)
                     slopes_x.append(after - before)
                     slopes_y.append(up - down)
@@ -528,9 +558,10 @@
             pltpu.VMEM((TILES, F, Z * X, LANES), F32),
             pltpu.VMEM((4, 512, 128), BF16), pltpu.VMEM((4, 768, 256), BF16),
             pltpu.VMEM((F, TILES, ROWS, LANES), F32), pltpu.VMEM((768, LANES), F32),
+            pltpu.VMEM((ROWS, LANES), F32), pltpu.VMEM((ROWS, LANES), F32),
         ] + [pltpu.VMEM((TILES + 1, ROWS, LANES), BF16)] * 4 + [
             pltpu.VMEM((2, ROWS, 384), F32),
-            pltpu.VMEM((7, F, X + 2, Z, LANES), F32), pltpu.VMEM((F, X + 2, Z, LANES), F32),
+            pltpu.VMEM((7, F, X + 2, Z, LANES), F32), pltpu.VMEM((X + 2, Z, LANES), F32),
             pltpu.VMEM((TILES, F, X * Z, LANES), F32), pltpu.VMEM((9, F * Z, LANES), F32),
         ] + [pltpu.VMEM((F, HALO * 8, Y), F32)] * 2 + [pltpu.VMEM((F, X, LANES), F32)] * 2
         + [pltpu.VMEM((F, HALO * 8, Y), F32)] * 2 + [pltpu.VMEM((F, X, LANES), F32)] * 2

time: 61.2 us -> 58.7 us (0.959)
  Pallas kernels: 60.3 us -> 57.8 us
    pallas_call x1, Pallas kernels: 47 us -> 44.5 us  [shards(): pl.pallas_call(main_kernel, out_shape=[shape((TILES, F, X * Z, LANES), F3...]
where the time goes in v3:
time: 58.7 us; the launch traced here: 58.5 us
  Pallas kernels  57.8 us (98%)
  between operations  0.66 us (1%)
    pallas_call x1, Pallas kernels, shards(): pl.pallas_call(main_kernel, out_shape=[shape((TILES, F, X * Z, LANES), F3...  44.5 us
    pallas_call x1, Pallas kernels, shards(): pl.pallas_call(scatter_kernel, out_shape=shape((F, Z * X, Y), F32), in_sp...  11.4 us
    pallas_call x1, Pallas kernels, shards(): pl.pallas_call(prepare_kernel, out_shape=shape((9, 8, LANES), I32), in_sp...  1.94 us

profile of v3, /device:TPU:0, one launch (start us, length us, event | category | flops | bytes accessed | tf_op | source)
XLA Modules:
  0.0 58.5 jit_solution(4237732931616232974)
XLA Ops:
  0.7 1.9 %prepare.1.info.info_hbm = s32[9,8,128]{2,1,0:T(8,128)} custom-call(s32[1]{0:T(128)S(6)} %copy.12.count_ref, s32[576]{0:T(1024)} %code_ref.3, s32[576]{0:T(1024)} %base_ref.3, s32[576]{0:T(1024)} %ghost_ref.1), custom_call_target="tpu_custom_call" | custom-call | tf_op jit(solution)/shard_map/prepare/pallas_call | solution.py:542
  2.6 44.5 %section.1 = (f32[4,5,512,128]{3,2,1,0:T(8,128)}, f32[9,40,128]{2,1,0:T(8,128)}, s32[9,8,128]{2,1,0:T(8,128)}) custom-call(f32[5,5]{1,0:T(8,128)} %flux_x.1, f32[5,5]{1,0:T(8,128)} %flux_y.1, s32[1]{0:T(128)S(6)} %copy.12.count_ref, s32[9,8,128]{2,1,0:T(8,128)} %prepare.1.info.info_hbm, f32[5,512,512]{2,1,0:T(8,128)} %bitcast.3, ...), custom_call_target="tpu_custom_call" | custom-call | tf_op jit(solution)/shard_map/section/pallas_call | solution.py:550
  47.1 11.4 %scatter.1 = f32[5,512,512]{2,1,0:T(8,128)} custom-call(s32[9,8,128]{2,1,0:T(8,128)} %get-tuple-element.8.info, f32[4,5,512,128]{3,2,1,0:T(8,128)} %get-tuple-element.9.section_hbm, f32[9,40,128]{2,1,0:T(8,128)} %get-tuple-element.10.arrived), custom_call_target="tpu_custom_call" | custom-call | tf_op jit(solution)/shard_map/scatter/pallas_call | solution.py:576

commit v4 on v3

--- a/solution.py
+++ b/solution.py
@@ -199,10 +199,10 @@
     for i, kind in enumerate(kinds):
         constant_copies.append(pltpu.make_async_copy(first_hbm.at[kind], firsts.at[i], sems.at[4 + i]))
         constant_copies.append(pltpu.make_async_copy(rest_hbm.at[kind], rests.at[i], sems.at[8 + i]))
-    for copy in copies + constant_copies:
+    for copy in [copies[0], copies[3], copies[1], copies[2]] + constant_copies:
         copy.start()
-    for copy in copies:
-        copy.wait()
+    copies[0].wait()
+    copies[3].wait()
     lane = lane_index()
     low_half = lane < 64
 
@@ -237,6 +237,9 @@
     ]
     for copy in side_copies:
         copy.start()
+
+    copies[1].wait()
+    copies[2].wait()
 
     def pack_rows(f, carry):
         for c in range(TILES):
@@ -453,9 +456,9 @@
         return carry
 
     written = []
-    for half in range(2):
-        lax.fori_loop(half * 4, half * 4 + 4, per_octet, 0)
-        rows = pl.ds(half * 256, 256)
+    for half in range(4):
+        lax.fori_loop(half * 2, half * 2 + 2, per_octet, 0)
+        rows = pl.ds(half * 128, 128)
         written.append(
             pltpu.make_async_copy(section_ref.at[:, :, rows], section_hbm.at[:, :, rows], out_sems.at[2 + half])
         )
@@ -567,7 +570,7 @@
         + [pltpu.VMEM((F, HALO * 8, Y), F32)] * 2 + [pltpu.VMEM((F, X, LANES), F32)] * 2
         + [pltpu.VMEM((F, 16, LANES), F32)] * 4
         + [pltpu.VMEM((4, REC, LANES), F32)]
-        + [dma((12,)), dma((2, F)), dma((2, F)), dma((15,)), dma((15,)), dma((9,)), dma((9,)), dma((4,))],
+        + [dma((12,)), dma((2, F)), dma((2, F)), dma((15,)), dma((15,)), dma((9,)), dma((9,)), dma((6,))],
         compiler_params=pltpu.CompilerParams(collective_id=0, has_side_effects=True, vmem_limit_bytes=VMEM_BYTES),
         name="section",
     )(

time: 58.7 us -> 58.4 us (level)
  no operation moved by 1% of the time
where the time goes in v4:
time: 58.4 us; the launch traced here: 58.1 us
  Pallas kernels  57.4 us (98%)
  between operations  0.66 us (1%)
    pallas_call x1, Pallas kernels, shards(): pl.pallas_call(main_kernel, out_shape=[shape((TILES, F, X * Z, LANES), F3...  44.2 us
    pallas_call x1, Pallas kernels, shards(): pl.pallas_call(scatter_kernel, out_shape=shape((F, Z * X, Y), F32), in_sp...  11.3 us
    pallas_call x1, Pallas kernels, shards(): pl.pallas_call(prepare_kernel, out_shape=shape((9, 8, LANES), I32), in_sp...  1.94 us

profile of v4, /device:TPU:0, one launch (start us, length us, event | category | flops | bytes accessed | tf_op | source)
XLA Modules:
  0.0 58.1 jit_solution(3063818719105756430)
XLA Ops:
  0.7 1.9 %prepare.1.info.info_hbm = s32[9,8,128]{2,1,0:T(8,128)} custom-call(s32[1]{0:T(128)S(6)} %copy.12.count_ref, s32[576]{0:T(1024)} %code_ref.3, s32[576]{0:T(1024)} %base_ref.3, s32[576]{0:T(1024)} %ghost_ref.1), custom_call_target="tpu_custom_call" | custom-call | tf_op jit(solution)/shard_map/prepare/pallas_call | solution.py:545
  2.6 44.2 %section.1 = (f32[4,5,512,128]{3,2,1,0:T(8,128)}, f32[9,40,128]{2,1,0:T(8,128)}, s32[9,8,128]{2,1,0:T(8,128)}) custom-call(f32[5,5]{1,0:T(8,128)} %flux_x.1, f32[5,5]{1,0:T(8,128)} %flux_y.1, s32[1]{0:T(128)S(6)} %copy.12.count_ref, s32[9,8,128]{2,1,0:T(8,128)} %prepare.1.info.info_hbm, f32[5,512,512]{2,1,0:T(8,128)} %bitcast.3, ...), custom_call_target="tpu_custom_call" | custom-call | tf_op jit(solution)/shard_map/section/pallas_call | solution.py:553
  46.8 11.3 %scatter.1 = f32[5,512,512]{2,1,0:T(8,128)} custom-call(s32[9,8,128]{2,1,0:T(8,128)} %get-tuple-element.8.info, f32[4,5,512,128]{3,2,1,0:T(8,128)} %get-tuple-element.9.section_hbm, f32[9,40,128]{2,1,0:T(8,128)} %get-tuple-element.10.arrived), custom_call_target="tpu_custom_call" | custom-call | tf_op jit(solution)/shard_map/scatter/pallas_call | solution.py:579
